TPU v7x, 256 devices: a whole 4x4x8 slice. The times are simulated.
256 devices in a mesh: ctx: 8 (over y, core), exp: 32 (over x, z).
Axes of the slice: x: 4, y: 4, z: 8, core: 2. Of those that a mesh axis runs over, the one named last changes fastest.
Arguments:
- tokens: bfloat16 [32, 1024, 2048], P('exp', 'ctx'), may hold values from -6 to 6
- input_gain: float32 [2048], replicated, may hold values from 0.1 to 1.9
- mixer_weight: bfloat16 [2048, 6144], P(None, 'ctx'), may hold values from -0.125 to 0.125
- rate_weight: bfloat16 [2048, 8, 4], P(None, 'ctx'), may hold values from -3 to 3
- conv_kernel: float32 [4, 8, 512], P(None, 'ctx'), may hold values from -3 to 3
- decay_scale: float32 [16], P('ctx'), may hold values from 0 to 0.05
- decay_bias: float32 [16], P('ctx'), may hold values from -3 to 3
- value_gain: float32 [128], replicated, may hold values from 0.1 to 1.9
- output_weight: bfloat16 [2048, 2048], P('ctx'), may hold values from -0.125 to 0.125
- start_state: float32 [16, 128, 128], P('ctx'), may hold values from -0.8 to 0.8
- post_gain: float32 [2048], replicated, may hold values from 0.1 to 1.9
- expert_gateup: bfloat16 [32, 2048, 1024], P('exp'), may hold values from -0.125 to 0.125
- expert_down: bfloat16 [32, 512, 2048], P('exp'), may hold values from -0.25 to 0.25
- route_ids: int32 [32, 1024, 4], P('exp', 'ctx'), may hold values from 0 to 31, all different within a row; in each aligned block of 128 rows (0 to 127, 128 to 255, ..., all dimensions but the last counted through in order) at most 20 rows name the same one
- route_weights: float32 [32, 1024, 4], P('exp', 'ctx'), may hold values from 0.05 to 0.5
Outputs:
- layer_out: float32 [32, 1024, 2048], P('exp', 'ctx')
- segment_states: float32 [32, 16, 128, 128], P('exp', 'ctx')
Inputs may be any that keep to these rules, and one draw needn't show every extreme that they name: `route_ids`: each token names 4 different experts. Within the 128 rows of one device (aligned blocks) no expert is named by more than 20 rows, a bound that some block reaches.
All inputs are finite; a program needn't handle non-finite values.
Results may differ from a plain program's by a relative error of at most 0.012.
Values may be sent and summed in bfloat16 or wider, within the bound.
No kernel may reach another device: no remote copies, remote signals or barrier semaphores. Data moves between devices by JAX's collectives and lax.ppermute only.
A program may use at most 128 MiB of HBM per device.

v0:
```python
import jax
import jax.numpy as jnp
from jax import lax
from jax.sharding import PartitionSpec as P

DK = 128
DV = 128
FFE = 512
KCONV = 4
HK = 8
HV = 16
BLOCK = 64
ROUTES = 4


EPSILON = 1e-06
highest = lax.Precision.HIGHEST


def passed_along(block, axis, distance):
    devices = range(lax.axis_size(axis))
    route = [(i - distance, i) for i in devices if i - distance in devices]
    return lax.ppermute(block, axis, route)


def rms_scale(values, scaling):
    widened = values.astype(jnp.float32)
    return (
        widened * lax.rsqrt(jnp.mean(widened * widened, axis=-1, keepdims=True) + EPSILON) * scaling
    )


def unit_rows(values):
    return values * lax.rsqrt(jnp.sum(values * values, axis=-1, keepdims=True) + EPSILON)


def lower_solve(strict_lower, right_side):
    result = right_side - jnp.einsum(
        "...ij,...jk->...ik", strict_lower, right_side, precision=highest
    )
    powered = strict_lower
    for _ in range((strict_lower.shape[-1] - 1).bit_length() - 1):
        powered = jnp.einsum("...ij,...jk->...ik", powered, powered, precision=highest)
        result = result + jnp.einsum("...ij,...jk->...ik", powered, result, precision=highest)
    return result


def short_conv(pre_conv, tail_rows, kernel):
    padded = jnp.concatenate([tail_rows, pre_conv], axis=0).astype(jnp.float32)
    length = pre_conv.shape[0]
    summed = jnp.zeros(pre_conv.shape, jnp.float32)
    for offset in range(kernel.shape[0]):
        summed = summed + kernel[offset] * padded[offset : offset + length]
    return jax.nn.silu(summed)


def to_blocks(array):
    moved = jnp.moveaxis(array, 1, 0)
    return moved.reshape((moved.shape[0], moved.shape[1] // BLOCK, BLOCK) + moved.shape[2:])


def head_inputs(activated, rate_rows, decay_scale, decay_bias):
    length = activated.shape[0]
    per_group = HV // HK
    head_count = activated.shape[1] * per_group
    queries = jnp.repeat(unit_rows(activated[..., :DK]) * DK ** (-0.5), per_group, axis=1)
    key_rows = jnp.repeat(unit_rows(activated[..., DK : 2 * DK]), per_group, axis=1)
    values = activated[..., 2 * DK :].reshape(length, head_count, DV)
    betas = jax.nn.sigmoid(rate_rows[..., :per_group].astype(jnp.float32)).reshape(
        length, head_count
    )
    decay_input = rate_rows[..., per_group:].astype(jnp.float32).reshape(length, head_count)
    decays = -decay_scale * jax.nn.softplus(decay_input + decay_bias)
    return (
        to_blocks(queries),
        to_blocks(key_rows),
        to_blocks(values),
        to_blocks(betas),
        to_blocks(decays),
    )


def block_terms(queries, key_rows, values, betas, decays):
    cumulative = jnp.cumsum(decays, axis=-1)
    row_index = jnp.arange(BLOCK)[:, None]
    col_index = jnp.arange(BLOCK)[None, :]
    decay_gaps = cumulative[..., :, None] - cumulative[..., None, :]
    causal = jnp.exp(jnp.where(row_index >= col_index, decay_gaps, -1e30))
    strict = jnp.where(row_index > col_index, causal, 0.0)
    key_gram = jnp.einsum("hncd,hnmd->hncm", key_rows, key_rows, precision=highest)
    strict_lower = betas[..., :, None] * key_gram * strict
    grown = jnp.exp(cumulative)[..., None]
    right_side = jnp.concatenate(
        [betas[..., None] * key_rows * grown, betas[..., None] * values], axis=-1
    )
    solved = lower_solve(strict_lower, right_side)
    wide_keys = solved[..., :DK]
    new_values = solved[..., DK:]
    scores = jnp.einsum("hncd,hnmd->hncm", queries, key_rows, precision=highest) * causal
    readers = queries * grown - jnp.einsum("hncm,hnmd->hncd", scores, wide_keys, precision=highest)
    local_out = jnp.einsum("hncm,hnme->hnce", scores, new_values, precision=highest)
    last_sum = cumulative[..., -1:]
    faded_keys = key_rows * jnp.exp(last_sum - cumulative)[..., None]
    identity = jnp.eye(DK, dtype=jnp.float32)
    transfer = jnp.exp(last_sum)[..., None] * identity - jnp.einsum(
        "hncd,hnce->hnde", faded_keys, wide_keys, precision=highest
    )
    inject = jnp.einsum("hncd,hnce->hnde", faded_keys, new_values, precision=highest)
    return (readers, local_out, transfer, inject)


def apply_state(readers, state):
    return jnp.einsum("hcd,hde->hce", readers, state, precision=highest)


def advance(transfer, state):
    return jnp.einsum("hde,hef->hdf", transfer, state, precision=highest)


def gate_norm(mixer_out, gate_part, value_gain):
    normed = (
        mixer_out
        * lax.rsqrt(jnp.mean(mixer_out * mixer_out, axis=-1, keepdims=True) + EPSILON)
        * value_gain
    )
    gated = normed * jax.nn.silu(gate_part.astype(jnp.float32))
    return gated.reshape(mixer_out.shape[0], -1).astype(jnp.bfloat16)


def body(
    tokens,
    input_gain,
    mixer_weight,
    rate_weight,
    conv_kernel,
    decay_scale,
    decay_bias,
    value_gain,
    output_weight,
    start_state,
    post_gain,
    expert_gateup,
    expert_down,
    route_ids,
    route_weights,
):
    own_rows = tokens[0]
    tok_rows = own_rows.shape[0]
    model_width = own_rows.shape[1]
    conv_width = 2 * DK + HV // HK * DV
    normed = rms_scale(own_rows, input_gain).astype(jnp.bfloat16)
    segment = lax.all_gather(normed, "ctx", axis=0, tiled=True)
    seg_rows = segment.shape[0]
    groups = rate_weight.shape[1]
    projected = (
        jnp.dot(segment, mixer_weight, preferred_element_type=jnp.float32)
        .astype(jnp.bfloat16)
        .reshape(seg_rows, groups, -1)
    )
    rate_rows = (
        jnp.dot(segment, rate_weight.reshape(model_width, -1), preferred_element_type=jnp.float32)
        .astype(jnp.bfloat16)
        .reshape(seg_rows, groups, -1)
    )
    pre_conv = projected[..., :conv_width]
    tail_rows = passed_along(pre_conv[seg_rows - (KCONV - 1) :], "exp", 1)
    activated = short_conv(pre_conv, tail_rows, conv_kernel)
    queries, key_rows, values, betas, decays = head_inputs(
        activated, rate_rows, decay_scale, decay_bias
    )
    readers, local_out, transfer, inject = block_terms(queries, key_rows, values, betas, decays)
    stacked = tuple(
        (jnp.moveaxis(member, 1, 0) for member in (readers, local_out, transfer, inject))
    )
    heads_here = readers.shape[0]
    zero_state = jnp.zeros((heads_here, DK, DV), jnp.float32)
    identity = jnp.broadcast_to(jnp.eye(DK, dtype=jnp.float32), (heads_here, DK, DK))

    def summary_step(carried, block_parts):
        partial_state, product = carried
        return (
            (
                advance(block_parts[2], partial_state) + block_parts[3],
                advance(block_parts[2], product),
            ),
            None,
        )

    (seg_inject, seg_transfer), _ = lax.scan(summary_step, (zero_state, identity), stacked)
    first_device = lax.axis_index("exp") == 0

    def relay_step(counter, arriving):
        passed = passed_along(advance(seg_transfer, arriving) + seg_inject, "exp", 1)
        return jnp.where(first_device, start_state, passed)

    incoming = lax.fori_loop(
        0, lax.axis_size("exp") - 1, relay_step, jnp.where(first_device, start_state, zero_state)
    )

    def second_step(carried, block_parts):
        out_rows = apply_state(block_parts[0], carried) + block_parts[1]
        return (advance(block_parts[2], carried) + block_parts[3], out_rows)

    final_state, outputs = lax.scan(second_step, incoming, stacked)
    mixer_out = jnp.moveaxis(outputs, 0, 1).reshape(heads_here, seg_rows, DV).transpose(1, 0, 2)
    gate_part = projected[..., conv_width:].reshape(seg_rows, heads_here, DV)
    gated = gate_norm(mixer_out, gate_part, value_gain)
    mixed = lax.psum_scatter(
        jnp.dot(gated, output_weight, preferred_element_type=jnp.float32),
        "ctx",
        scatter_dimension=0,
        tiled=True,
    )
    hidden_state = own_rows.astype(jnp.float32) + mixed
    post = rms_scale(hidden_state, post_gain).astype(jnp.bfloat16)
    expert_count = lax.axis_size("exp")
    capacity = 5 * tok_rows * ROUTES // (4 * expert_count)
    id_list = route_ids[0].reshape(-1)
    onehot = (id_list[:, None] == jnp.arange(expert_count, dtype=jnp.int32)[None, :]).astype(
        jnp.int32
    )
    slots = jnp.sum((jnp.cumsum(onehot, axis=0) - onehot) * onehot, axis=1)
    destination = id_list * capacity + slots
    token_index = jnp.arange(tok_rows * ROUTES, dtype=jnp.int32) // ROUTES
    source_row = jnp.zeros(expert_count * capacity, jnp.int32).at[destination].set(token_index)
    filled = (
        jnp.zeros(expert_count * capacity, jnp.bfloat16)
        .at[destination]
        .set(jnp.ones(tok_rows * ROUTES, jnp.bfloat16))
    )
    outgoing = (post[source_row] * filled[:, None]).reshape(expert_count, capacity, model_width)
    arrived = lax.all_to_all(outgoing, "exp", split_axis=0, concat_axis=0, tiled=True)
    flat_rows = arrived.reshape(-1, model_width)
    gate_up = jnp.dot(flat_rows, expert_gateup[0], preferred_element_type=jnp.float32)
    expert_hidden = (jax.nn.silu(gate_up[:, :FFE]) * gate_up[:, FFE:]).astype(jnp.bfloat16)
    expert_out = jnp.dot(expert_hidden, expert_down[0], preferred_element_type=jnp.float32).astype(
        jnp.bfloat16
    )
    returned = lax.all_to_all(
        expert_out.reshape(arrived.shape), "exp", split_axis=0, concat_axis=0, tiled=True
    )
    picked = returned.reshape(expert_count * capacity, model_width)[destination].reshape(
        tok_rows, ROUTES, model_width
    )
    routed = jnp.sum(route_weights[0][..., None] * picked.astype(jnp.float32), axis=1)
    layer_out = hidden_state + routed
    return (layer_out[None], final_state[None])


def solution(mesh):
    in_specs = (
        P("exp", "ctx", None),
        P(),
        P(None, "ctx"),
        P(None, "ctx", None),
        P(None, "ctx", None),
        P("ctx"),
        P("ctx"),
        P(),
        P("ctx", None),
        P("ctx", None, None),
        P(),
        P("exp", None, None),
        P("exp", None, None),
        P("exp", "ctx", None),
        P("exp", "ctx", None),
    )
    out_specs = (P("exp", "ctx", None), P("exp", "ctx", None, None))
    return jax.shard_map(body, mesh=mesh, in_specs=in_specs, out_specs=out_specs, check_vma=False)
```

profile of v0, /device:TPU:24, one launch (start us, length us, event | category | flops | bytes accessed | tf_op | source)
XLA Modules:
  0.0 749.0 jit_solution(10715073160736058607)
XLA Ops:
  13.3 33.1 %all-gather.2.cloned.1.call-done = bf16[1024,2048]{1,0:T(8,128)(2,1)} async-done(((bf16[128,2048]{1,0:T(8,128)(2,1)}), bf16[1024,2048]{1,0:T(8,128)(2,1)}) %all-gather.2.cloned.1.call-update) | async-done | bytes 4194320 | tf_op jit(solution)/shard_map/all_gather | solution.py:152
  46.3 5.7 fusion.31
  101.5 4.0 convolution_bitcast_fusion
  107.0 4.0 bitcast_subtract_fusion
  111.1 24.2 %while.37 = (s32[]{:T(128)}, f32[2,128,128]{2,1,0:T(8,128)S(1)}, f32[2,128,128]{2,1,0:T(8,128)S(1)}, f32[16,2,128,128]{3,2,1,0:T(8,128)S(1)}, f32[16,2,128,128]{3,2,1,0:T(8,128)}, /*index=5*/s32[]{:T(128)}, s32[]{:T(128)}) while((s32[]{:T(128)}, f32[2,128,128]{2,1,0:T(8,128)S(1)}, f32[2,128,128]{2,1,0:T(8,128)S(1)}, ...), condition=%wide.region_4.5_spmd.clone, body=%wide.region_3.4_spmd.clone.sunk | while | flops 100728832 | bytes 1442907 | solution.py:189
  135.3 267.1 %while.35 = (s32[]{:T(128)}, f32[2,128,128]{2,1,0:T(8,128)S(1)}, pred[]{:T(512)}, f32[2,128,128]{2,1,0:T(8,128)S(1)}, f32[2,128,128]{2,1,0:T(8,128)S(1)}, /*index=5*/f32[2,128,128]{2,1,0:T(8,128)S(1)}, s32[]{:T(128)}) while((s32[]{:T(128)}, f32[2,128,128]{2,1,0:T(8,128)S(1)}, pred[]{:T(512)}, f32[2,128,128]{2,1,0:T(8,128)S(1)}, ...), condition=%wide.region_6.7_spmd, body=%wide.region_5.6_spmd.sunk | while | flops 50397184 | bytes 1441910 | solution.py:196
  142.2 4.4 collective-permute-start
  149.4 4.4 collective-permute-start
  156.6 4.4 collective-permute-start
  163.8 4.4 collective-permute-start
  170.9 4.4 collective-permute-start
  178.2 5.6 collective-permute-start
  187.4 6.1 collective-permute-start
  197.1 5.7 collective-permute-start
  205.6 5.1 collective-permute-start
  213.5 5.6 collective-permute-start
  221.9 5.6 collective-permute-start
  230.3 5.6 collective-permute-start
  238.7 5.7 collective-permute-start
  248.4 6.1 collective-permute-start
  257.9 5.3 collective-permute-start
  266.0 5.1 collective-permute-start
  273.9 5.6 collective-permute-start
  282.3 5.6 collective-permute-start
  290.7 5.6 collective-permute-start
  299.1 6.8 collective-permute-start
  308.7 5.9 collective-permute-start
  317.4 6.5 collective-permute-start
  326.7 6.9 collective-permute-start
  337.6 6.8 collective-permute-start
  347.6 6.3 collective-permute-start
  356.7 6.8 collective-permute-start
  366.3 6.3 collective-permute-start
  375.4 6.2 collective-permute-start
  384.4 6.2 collective-permute-start
  393.4 6.5 collective-permute-start
  402.4 47.4 %while.36 = (s32[]{:T(128)}, f32[2,128,128]{2,1,0:T(8,128)S(1)}, f32[16,2,64,128]{3,2,0,1:T(8,128)}, f32[16,2,128,128]{3,2,1,0:T(8,128)S(1)}, f32[16,2,128,128]{...) while((s32[]{:T(128)}, f32[2,128,128]{2,1,0:T(8,128)S(1)}, ...), condition=%wide.region_9.10_spmd, body=%wide.region_8.9_spmd.sunk | while | flops 75546624 | bytes 1116245 | solution.py:204
  453.7 4.5 fusion.88
  463.5 4.0 scatter_custom_fusion.1
  467.7 66.7 %reduce-scatter.2.cloned.1.call-done = f32[128,2048]{1,0:T(8,128)} async-done(((f32[1024,2048]{1,0:T(8,128)}), f32[128,2048]{1,0:T(8,128)}) %reduce-scatter.2.cloned.1.call-update) | async-done | bytes 1048592 | tf_op jit(solution)/shard_map/reduce_scatter | solution.py:208
  536.2 4.1 gather_fusion
  540.3 5.2 gather.9
  547.6 83.4 %all_to_all.10 = bf16[32,20,2048]{2,1,0:T(8,128)(2,1)} all-to-all(bf16[32,20,2048]{2,1,0:T(8,128)(2,1)S(1)} %broadcast_multiply_fusion), channel_id=1, replica_groups=mesh['ctx'=8,'exp'=32] {'exp'}, dimensions={0} | all-to-all | bytes 5242880 | tf_op jit(solution)/shard_map/all_to_all | solution.py:232
  634.7 4.8 fusion.19
  643.5 5.6 all-to-all-start.1
  649.2 74.0 %all-to-all-done.1 = bf16[32,20,2048]{2,1,0:T(8,128)(2,1)} async-done(((bf16[32,20,2048]{2,1,0:T(8,128)(2,1)}), bf16[32,20,2048]{2,1,0:T(8,128)(2,1)}, u32[]{:S(2)}, u32[]{:S(2)}) %all-to-all-start.1) | async-done | bytes 2621472 | tf_op jit(solution)/shard_map/all_to_all | solution.py:239
  730.2 4.7 reshape.241
  734.9 5.6 multiply_reduce_fusion
  (366 shorter events, 250.7 us)
Async XLA Ops:
  7.2 39.2 %copy-start = (bf16[2048,768]{1,0:T(8,128)(2,1)S(1)}, bf16[2048,768]{1,0:T(8,128)(2,1)}, u32[]{:S(2)}) copy-start(bf16[2048,768]{1,0:T(8,128)(2,1)} %param.23) | copy-start | bytes 9437188
  7.2 5.4 copy-start.26
  7.2 6.0 copy-start.10
  7.2 39.1 %all-gather.2.cloned.1.call-start = ((), (), s32[]{:S(2)}) async-start(), calls=%async_computation.3 | async-start | bytes 4718592 | tf_op jit(solution)/shard_map/all_gather | solution.py:152
  10.7 523.7 %reduce-scatter.2.cloned.1.call-start = ((), (), s32[]{:S(2)}) async-start(), calls=%async_computation.4 | async-start | bytes 9437184 | tf_op jit(solution)/shard_map/reduce_scatter | solution.py:208
  13.3 42.8 %copy-start.19 = (bf16[2048,1,4]{0,2,1:T(4,128)(2,1)S(1)}, bf16[2048,1,4]{0,2,1:T(4,128)(2,1)}, u32[]{:S(2)}) copy-start(bf16[2048,1,4]{0,2,1:T(4,128)(2,1)} %param.24) | copy-start | bytes 49156
  46.3 9.7 %copy-start.9 = (bf16[1024,2048]{1,0:T(8,128)(2,1)S(1)}, bf16[1024,2048]{1,0:T(8,128)(2,1)}, u32[]{:S(2)}) copy-start(bf16[1024,2048]{1,0:T(8,128)(2,1)} %all-gather.2.cloned.1.call-done) | copy-start | bytes 12582916
  52.1 5.1 copy-start.11
  52.2 11.6 %collective-permute-start.1 = (bf16[3,1,512]{2,0,1:T(4,128)(2,1)S(1)}, bf16[3,1,512]{2,0,1:T(4,128)(2,1)S(1)}, u32[]{:S(2)}, u32[]{:S(2)}) collective-permute-start(bf16[3,1,512]{2,0,1:T(4,128)(2,1)S(1)} %slice.99), channel_id=1, source_target_pairs={{0,1},{1,2},{2,3},{3,4},{4,5},{5,6},{6,7},{7,8},{8,9},{9,10},{10,1... | collective-permute-start | bytes 9224 | tf_op jit(solution)/shard_map/ppermute | solution.py:23
  135.5 6.3 collective-permute-start
  142.2 6.9 collective-permute-start
  149.4 6.9 collective-permute-start
  156.6 6.9 collective-permute-start
  163.8 6.9 collective-permute-start
  170.9 6.9 collective-permute-start
  178.2 9.0 %collective-permute-start = (f32[2,128,128]{2,1,0:T(8,128)S(1)}, f32[2,128,128]{2,1,0:T(8,128)S(1)}, u32[]{:S(2)}, u32[]{:S(2)}) collective-permute-start(f32[2,128,128]{2,1,0:T(8,128)S(1)} %convolution_add_fusion.10), channel_id=1, source_target_pairs={{0,1},{1,2},{2,3},{3,4},{4,5},{5,6},{6,7},{7,8},{8,9},{9,10},{10,1... | collective-permute-start | bytes 393224 | tf_op jit(solution)/shard_map/while/body/eval_jaxpr/ppermute | solution.py:23
  187.4 9.3 %collective-permute-start = (f32[2,128,128]{2,1,0:T(8,128)S(1)}, f32[2,128,128]{2,1,0:T(8,128)S(1)}, u32[]{:S(2)}, u32[]{:S(2)}) collective-permute-start(f32[2,128,128]{2,1,0:T(8,128)S(1)} %convolution_add_fusion.10), channel_id=1, source_target_pairs={{0,1},{1,2},{2,3},{3,4},{4,5},{5,6},{6,7},{7,8},{8,9},{9,10},{10,1... | collective-permute-start | bytes 393224 | tf_op jit(solution)/shard_map/while/body/eval_jaxpr/ppermute | solution.py:23
  197.1 8.2 %collective-permute-start = (f32[2,128,128]{2,1,0:T(8,128)S(1)}, f32[2,128,128]{2,1,0:T(8,128)S(1)}, u32[]{:S(2)}, u32[]{:S(2)}) collective-permute-start(f32[2,128,128]{2,1,0:T(8,128)S(1)} %convolution_add_fusion.10), channel_id=1, source_target_pairs={{0,1},{1,2},{2,3},{3,4},{4,5},{5,6},{6,7},{7,8},{8,9},{9,10},{10,1... | collective-permute-start | bytes 393224 | tf_op jit(solution)/shard_map/while/body/eval_jaxpr/ppermute | solution.py:23
  205.6 7.6 %collective-permute-start = (f32[2,128,128]{2,1,0:T(8,128)S(1)}, f32[2,128,128]{2,1,0:T(8,128)S(1)}, u32[]{:S(2)}, u32[]{:S(2)}) collective-permute-start(f32[2,128,128]{2,1,0:T(8,128)S(1)} %convolution_add_fusion.10), channel_id=1, source_target_pairs={{0,1},{1,2},{2,3},{3,4},{4,5},{5,6},{6,7},{7,8},{8,9},{9,10},{10,1... | collective-permute-start | bytes 393224 | tf_op jit(solution)/shard_map/while/body/eval_jaxpr/ppermute | solution.py:23
  213.5 8.1 %collective-permute-start = (f32[2,128,128]{2,1,0:T(8,128)S(1)}, f32[2,128,128]{2,1,0:T(8,128)S(1)}, u32[]{:S(2)}, u32[]{:S(2)}) collective-permute-start(f32[2,128,128]{2,1,0:T(8,128)S(1)} %convolution_add_fusion.10), channel_id=1, source_target_pairs={{0,1},{1,2},{2,3},{3,4},{4,5},{5,6},{6,7},{7,8},{8,9},{9,10},{10,1... | collective-permute-start | bytes 393224 | tf_op jit(solution)/shard_map/while/body/eval_jaxpr/ppermute | solution.py:23
  221.9 8.1 %collective-permute-start = (f32[2,128,128]{2,1,0:T(8,128)S(1)}, f32[2,128,128]{2,1,0:T(8,128)S(1)}, u32[]{:S(2)}, u32[]{:S(2)}) collective-permute-start(f32[2,128,128]{2,1,0:T(8,128)S(1)} %convolution_add_fusion.10), channel_id=1, source_target_pairs={{0,1},{1,2},{2,3},{3,4},{4,5},{5,6},{6,7},{7,8},{8,9},{9,10},{10,1... | collective-permute-start | bytes 393224 | tf_op jit(solution)/shard_map/while/body/eval_jaxpr/ppermute | solution.py:23
  230.3 8.1 %collective-permute-start = (f32[2,128,128]{2,1,0:T(8,128)S(1)}, f32[2,128,128]{2,1,0:T(8,128)S(1)}, u32[]{:S(2)}, u32[]{:S(2)}) collective-permute-start(f32[2,128,128]{2,1,0:T(8,128)S(1)} %convolution_add_fusion.10), channel_id=1, source_target_pairs={{0,1},{1,2},{2,3},{3,4},{4,5},{5,6},{6,7},{7,8},{8,9},{9,10},{10,1... | collective-permute-start | bytes 393224 | tf_op jit(solution)/shard_map/while/body/eval_jaxpr/ppermute | solution.py:23
  238.7 9.3 %collective-permute-start = (f32[2,128,128]{2,1,0:T(8,128)S(1)}, f32[2,128,128]{2,1,0:T(8,128)S(1)}, u32[]{:S(2)}, u32[]{:S(2)}) collective-permute-start(f32[2,128,128]{2,1,0:T(8,128)S(1)} %convolution_add_fusion.10), channel_id=1, source_target_pairs={{0,1},{1,2},{2,3},{3,4},{4,5},{5,6},{6,7},{7,8},{8,9},{9,10},{10,1... | collective-permute-start | bytes 393224 | tf_op jit(solution)/shard_map/while/body/eval_jaxpr/ppermute | solution.py:23
  248.4 9.2 %collective-permute-start = (f32[2,128,128]{2,1,0:T(8,128)S(1)}, f32[2,128,128]{2,1,0:T(8,128)S(1)}, u32[]{:S(2)}, u32[]{:S(2)}) collective-permute-start(f32[2,128,128]{2,1,0:T(8,128)S(1)} %convolution_add_fusion.10), channel_id=1, source_target_pairs={{0,1},{1,2},{2,3},{3,4},{4,5},{5,6},{6,7},{7,8},{8,9},{9,10},{10,1... | collective-permute-start | bytes 393224 | tf_op jit(solution)/shard_map/while/body/eval_jaxpr/ppermute | solution.py:23
  257.9 7.8 %collective-permute-start = (f32[2,128,128]{2,1,0:T(8,128)S(1)}, f32[2,128,128]{2,1,0:T(8,128)S(1)}, u32[]{:S(2)}, u32[]{:S(2)}) collective-permute-start(f32[2,128,128]{2,1,0:T(8,128)S(1)} %convolution_add_fusion.10), channel_id=1, source_target_pairs={{0,1},{1,2},{2,3},{3,4},{4,5},{5,6},{6,7},{7,8},{8,9},{9,10},{10,1... | collective-permute-start | bytes 393224 | tf_op jit(solution)/shard_map/while/body/eval_jaxpr/ppermute | solution.py:23
  266.0 7.6 %collective-permute-start = (f32[2,128,128]{2,1,0:T(8,128)S(1)}, f32[2,128,128]{2,1,0:T(8,128)S(1)}, u32[]{:S(2)}, u32[]{:S(2)}) collective-permute-start(f32[2,128,128]{2,1,0:T(8,128)S(1)} %convolution_add_fusion.10), channel_id=1, source_target_pairs={{0,1},{1,2},{2,3},{3,4},{4,5},{5,6},{6,7},{7,8},{8,9},{9,10},{10,1... | collective-permute-start | bytes 393224 | tf_op jit(solution)/shard_map/while/body/eval_jaxpr/ppermute | solution.py:23
  273.9 8.1 %collective-permute-start = (f32[2,128,128]{2,1,0:T(8,128)S(1)}, f32[2,128,128]{2,1,0:T(8,128)S(1)}, u32[]{:S(2)}, u32[]{:S(2)}) collective-permute-start(f32[2,128,128]{2,1,0:T(8,128)S(1)} %convolution_add_fusion.10), channel_id=1, source_target_pairs={{0,1},{1,2},{2,3},{3,4},{4,5},{5,6},{6,7},{7,8},{8,9},{9,10},{10,1... | collective-permute-start | bytes 393224 | tf_op jit(solution)/shard_map/while/body/eval_jaxpr/ppermute | solution.py:23
  282.3 8.1 %collective-permute-start = (f32[2,128,128]{2,1,0:T(8,128)S(1)}, f32[2,128,128]{2,1,0:T(8,128)S(1)}, u32[]{:S(2)}, u32[]{:S(2)}) collective-permute-start(f32[2,128,128]{2,1,0:T(8,128)S(1)} %convolution_add_fusion.10), channel_id=1, source_target_pairs={{0,1},{1,2},{2,3},{3,4},{4,5},{5,6},{6,7},{7,8},{8,9},{9,10},{10,1... | collective-permute-start | bytes 393224 | tf_op jit(solution)/shard_map/while/body/eval_jaxpr/ppermute | solution.py:23
  290.7 8.1 %collective-permute-start = (f32[2,128,128]{2,1,0:T(8,128)S(1)}, f32[2,128,128]{2,1,0:T(8,128)S(1)}, u32[]{:S(2)}, u32[]{:S(2)}) collective-permute-start(f32[2,128,128]{2,1,0:T(8,128)S(1)} %convolution_add_fusion.10), channel_id=1, source_target_pairs={{0,1},{1,2},{2,3},{3,4},{4,5},{5,6},{6,7},{7,8},{8,9},{9,10},{10,1... | collective-permute-start | bytes 393224 | tf_op jit(solution)/shard_map/while/body/eval_jaxpr/ppermute | solution.py:23
  299.1 9.3 %collective-permute-start = (f32[2,128,128]{2,1,0:T(8,128)S(1)}, f32[2,128,128]{2,1,0:T(8,128)S(1)}, u32[]{:S(2)}, u32[]{:S(2)}) collective-permute-start(f32[2,128,128]{2,1,0:T(8,128)S(1)} %convolution_add_fusion.10), channel_id=1, source_target_pairs={{0,1},{1,2},{2,3},{3,4},{4,5},{5,6},{6,7},{7,8},{8,9},{9,10},{10,1... | collective-permute-start | bytes 393224 | tf_op jit(solution)/shard_map/while/body/eval_jaxpr/ppermute | solution.py:23
  308.7 8.4 %collective-permute-start = (f32[2,128,128]{2,1,0:T(8,128)S(1)}, f32[2,128,128]{2,1,0:T(8,128)S(1)}, u32[]{:S(2)}, u32[]{:S(2)}) collective-permute-start(f32[2,128,128]{2,1,0:T(8,128)S(1)} %convolution_add_fusion.10), channel_id=1, source_target_pairs={{0,1},{1,2},{2,3},{3,4},{4,5},{5,6},{6,7},{7,8},{8,9},{9,10},{10,1... | collective-permute-start | bytes 393224 | tf_op jit(solution)/shard_map/while/body/eval_jaxpr/ppermute | solution.py:23
  317.4 9.0 %collective-permute-start = (f32[2,128,128]{2,1,0:T(8,128)S(1)}, f32[2,128,128]{2,1,0:T(8,128)S(1)}, u32[]{:S(2)}, u32[]{:S(2)}) collective-permute-start(f32[2,128,128]{2,1,0:T(8,128)S(1)} %convolution_add_fusion.10), channel_id=1, source_target_pairs={{0,1},{1,2},{2,3},{3,4},{4,5},{5,6},{6,7},{7,8},{8,9},{9,10},{10,1... | collective-permute-start | bytes 393224 | tf_op jit(solution)/shard_map/while/body/eval_jaxpr/ppermute | solution.py:23
  326.7 10.6 %collective-permute-start = (f32[2,128,128]{2,1,0:T(8,128)S(1)}, f32[2,128,128]{2,1,0:T(8,128)S(1)}, u32[]{:S(2)}, u32[]{:S(2)}) collective-permute-start(f32[2,128,128]{2,1,0:T(8,128)S(1)} %convolution_add_fusion.10), channel_id=1, source_target_pairs={{0,1},{1,2},{2,3},{3,4},{4,5},{5,6},{6,7},{7,8},{8,9},{9,10},{10,1... | collective-permute-start | bytes 393224 | tf_op jit(solution)/shard_map/while/body/eval_jaxpr/ppermute | solution.py:23
  337.6 9.6 %collective-permute-start = (f32[2,128,128]{2,1,0:T(8,128)S(1)}, f32[2,128,128]{2,1,0:T(8,128)S(1)}, u32[]{:S(2)}, u32[]{:S(2)}) collective-permute-start(f32[2,128,128]{2,1,0:T(8,128)S(1)} %convolution_add_fusion.10), channel_id=1, source_target_pairs={{0,1},{1,2},{2,3},{3,4},{4,5},{5,6},{6,7},{7,8},{8,9},{9,10},{10,1... | collective-permute-start | bytes 393224 | tf_op jit(solution)/shard_map/while/body/eval_jaxpr/ppermute | solution.py:23
  347.6 8.8 %collective-permute-start = (f32[2,128,128]{2,1,0:T(8,128)S(1)}, f32[2,128,128]{2,1,0:T(8,128)S(1)}, u32[]{:S(2)}, u32[]{:S(2)}) collective-permute-start(f32[2,128,128]{2,1,0:T(8,128)S(1)} %convolution_add_fusion.10), channel_id=1, source_target_pairs={{0,1},{1,2},{2,3},{3,4},{4,5},{5,6},{6,7},{7,8},{8,9},{9,10},{10,1... | collective-permute-start | bytes 393224 | tf_op jit(solution)/shard_map/while/body/eval_jaxpr/ppermute | solution.py:23
  356.7 9.3 %collective-permute-start = (f32[2,128,128]{2,1,0:T(8,128)S(1)}, f32[2,128,128]{2,1,0:T(8,128)S(1)}, u32[]{:S(2)}, u32[]{:S(2)}) collective-permute-start(f32[2,128,128]{2,1,0:T(8,128)S(1)} %convolution_add_fusion.10), channel_id=1, source_target_pairs={{0,1},{1,2},{2,3},{3,4},{4,5},{5,6},{6,7},{7,8},{8,9},{9,10},{10,1... | collective-permute-start | bytes 393224 | tf_op jit(solution)/shard_map/while/body/eval_jaxpr/ppermute | solution.py:23
  366.3 8.8 %collective-permute-start = (f32[2,128,128]{2,1,0:T(8,128)S(1)}, f32[2,128,128]{2,1,0:T(8,128)S(1)}, u32[]{:S(2)}, u32[]{:S(2)}) collective-permute-start(f32[2,128,128]{2,1,0:T(8,128)S(1)} %convolution_add_fusion.10), channel_id=1, source_target_pairs={{0,1},{1,2},{2,3},{3,4},{4,5},{5,6},{6,7},{7,8},{8,9},{9,10},{10,1... | collective-permute-start | bytes 393224 | tf_op jit(solution)/shard_map/while/body/eval_jaxpr/ppermute | solution.py:23
  375.4 8.7 %collective-permute-start = (f32[2,128,128]{2,1,0:T(8,128)S(1)}, f32[2,128,128]{2,1,0:T(8,128)S(1)}, u32[]{:S(2)}, u32[]{:S(2)}) collective-permute-start(f32[2,128,128]{2,1,0:T(8,128)S(1)} %convolution_add_fusion.10), channel_id=1, source_target_pairs={{0,1},{1,2},{2,3},{3,4},{4,5},{5,6},{6,7},{7,8},{8,9},{9,10},{10,1... | collective-permute-start | bytes 393224 | tf_op jit(solution)/shard_map/while/body/eval_jaxpr/ppermute | solution.py:23
  384.4 8.7 %collective-permute-start = (f32[2,128,128]{2,1,0:T(8,128)S(1)}, f32[2,128,128]{2,1,0:T(8,128)S(1)}, u32[]{:S(2)}, u32[]{:S(2)}) collective-permute-start(f32[2,128,128]{2,1,0:T(8,128)S(1)} %convolution_add_fusion.10), channel_id=1, source_target_pairs={{0,1},{1,2},{2,3},{3,4},{4,5},{5,6},{6,7},{7,8},{8,9},{9,10},{10,1... | collective-permute-start | bytes 393224 | tf_op jit(solution)/shard_map/while/body/eval_jaxpr/ppermute | solution.py:23
  393.4 9.0 %collective-permute-start = (f32[2,128,128]{2,1,0:T(8,128)S(1)}, f32[2,128,128]{2,1,0:T(8,128)S(1)}, u32[]{:S(2)}, u32[]{:S(2)}) collective-permute-start(f32[2,128,128]{2,1,0:T(8,128)S(1)} %convolution_add_fusion.10), channel_id=1, source_target_pairs={{0,1},{1,2},{2,3},{3,4},{4,5},{5,6},{6,7},{7,8},{8,9},{9,10},{10,1... | collective-permute-start | bytes 393224 | tf_op jit(solution)/shard_map/while/body/eval_jaxpr/ppermute | solution.py:23
  402.4 49.1 %copy-start.32 = (f32[128]{0:T(128)S(1)}, f32[128]{0:T(128)}, u32[]{:S(2)}) copy-start(f32[128]{0:T(128)} %param.28) | copy-start | bytes 1540
  458.2 76.2 %copy-start.3 = (bf16[1,128,2048]{2,1,0:T(8,128)(2,1)S(1)}, bf16[1,128,2048]{2,1,0:T(8,128)(2,1)}, u32[]{:S(2)}) copy-start(bf16[1,128,2048]{2,1,0:T(8,128)(2,1)} %param.21) | copy-start | bytes 1572868
  458.9 77.0 %copy-start.20 = (f32[2048]{0:T(1024)S(1)}, f32[2048]{0:T(1024)}, u32[]{:S(2)}) copy-start(f32[2048]{0:T(1024)} %param.31) | copy-start | bytes 24580
  643.5 5.6 copy-start.29
  643.5 79.7 %all-to-all-start.1 = ((bf16[32,20,2048]{2,1,0:T(8,128)(2,1)}), bf16[32,20,2048]{2,1,0:T(8,128)(2,1)}, u32[]{:S(2)}, u32[]{:S(2)}) async-start(bf16[32,20,2048]{2,1,0:T(8,128)(2,1)} %reshape.235), calls=%async_computation.2 | async-start | bytes 6291456 | tf_op jit(solution)/shard_map/all_to_all | solution.py:239
  734.9 5.6 copy-start.4
  734.9 5.6 copy-start.8
  734.9 6.8 copy-start.1
  (22 other events, 52.5 us)
Sparse Core Ops, SparseCore 0:
  10.8 35.4 all-gather.1
  458.4 75.9 reduce-scatter.1
where the time goes:
time: 757 us; the launch traced here: 749 us
  waiting for transfers between devices  256 us (34%)
  starting transfers between devices  184 us (24%)
  matrix products  130 us (17%)
  blocking collectives  83.4 us (11%)
  local copies, waits for them, and re-layouts  49.8 us (7%)
  other arithmetic  27.2 us (4%)
  between operations  15.3 us (2%)
    ppermute x32, starting transfers between devices, passed_along(): return lax.ppermute(block, axis, route)  178 us
    all_to_all x1, blocking collectives, body(): lax.all_to_all(outgoing, 'exp', split_axis=0, concat_axis=0, tiled=True)  83.4 us
    ppermute x32, waiting for transfers between devices, passed_along(): return lax.ppermute(block, axis, route)  82.6 us
    all_to_all x1, waiting for transfers between devices, body(): lax.all_to_all(expert_out.reshape(arrived.shape), 'exp', split_axis=0, co...  74 us
    reduce_scatter x1, waiting for transfers between devices, body(): lax.psum_scatter(jnp.dot(gated, output_weight, preferred_element_type=jnp...  66.7 us
    dot_general x79, matrix products, advance(): return jnp.einsum('hde,hef->hdf', transfer, state, precision=highest)  50 us
    all_gather x1, waiting for transfers between devices, body(): segment = lax.all_gather(normed, 'ctx', axis=0, tiled=True)  33.1 us
    dot_general x16, matrix products, apply_state(): return jnp.einsum('hcd,hde->hce', readers, state, precision=highest)  28 us
  transfers between devices with their start and end apart: 35, of which 34 were waited for; matrix products, arithmetic and copies ran while one was open for 3% of the time, Pallas kernels for 0%

commit v1 on v0

v1 whole, which is shorter than its diff:
```python
import functools

import jax
import jax.numpy as jnp
from jax import lax
from jax.experimental import pallas as pl
from jax.experimental.pallas import tpu as pltpu
from jax.sharding import Mesh
from jax.sharding import PartitionSpec as P

DK = 128
DV = 128
FFE = 512
HEADS = 2
ROUTES = 4
CHUNK = 128
EPSILON = 1e-06
CTX = ("y", "core")
EXP = ("x", "z")
bf16 = jnp.bfloat16
f32 = jnp.float32
highest = lax.Precision.HIGHEST
VMEM = pl.BlockSpec(memory_space=pltpu.VMEM)
SMEM = pl.BlockSpec(memory_space=pltpu.SMEM)
GRANT = 56 * 1024 * 1024


def mm(a, b):
    return jnp.dot(a.astype(bf16), b.astype(bf16), preferred_element_type=f32)


def mm_t(a, b):
    return lax.dot_general(
        a.astype(bf16), b.astype(bf16), (((1,), (1,)), ((), ())), preferred_element_type=f32
    )


def rms_scale(values, scaling):
    widened = values.astype(f32)
    return (
        widened * lax.rsqrt(jnp.mean(widened * widened, axis=-1, keepdims=True) + EPSILON) * scaling
    )


def unit_rows(values):
    return values * lax.rsqrt(jnp.sum(values * values, axis=-1, keepdims=True) + EPSILON)


def silu(values):
    return values / (1.0 + jnp.exp(-values))


def square_iota(size, axis):
    return lax.broadcasted_iota(jnp.int32, (size, size), axis)


def delta_kernel(
    seg_ref, halo_ref, weight_ref, conv_ref, rate_par_ref,
    gate_ref, reader_ref, local_ref, summary_ref, packed_ref,
    rows_scr, rate_scr,
):
    seg_rows = seg_ref.shape[0]
    width = conv_ref.shape[1]
    steps = seg_rows // CHUNK

    def project(rows):
        return jnp.dot(rows, weight_ref[...], preferred_element_type=f32).astype(bf16)

    rows_scr[0:8, :] = project(halo_ref[...])[:, :width].astype(f32)

    def project_step(i, _):
        at = pl.multiple_of(i * CHUNK, CHUNK)
        made = project(seg_ref[pl.ds(at, CHUNK), :])
        rows_scr[pl.ds(pl.multiple_of(at + 8, 8), CHUNK), :] = made[:, :width].astype(f32)
        gate_ref[pl.ds(at, CHUNK), :] = made[:, width : width + HEADS * DV]
        rate_scr[pl.ds(at, CHUNK), :] = made[:, width + HEADS * DV :].astype(f32)
        return 0

    lax.fori_loop(0, steps, project_step, 0)

    row = square_iota(CHUNK, 0)
    col = square_iota(CHUNK, 1)
    lower = (row >= col).astype(f32)
    eye = (row == col).astype(f32)
    for h in range(HEADS):
        summary_ref[h, :, :DK] = eye
        summary_ref[h, :, DK:] = jnp.zeros((DK, DV), f32)

    pair = 2

    def chunk_step(i, _):
        units = []
        for u in range(pair):
            at = pl.multiple_of((i * pair + u) * CHUNK, CHUNK)
            window = rows_scr[pl.ds(at, CHUNK + 8), :]
            summed = conv_ref[0:1, :] * window[5 : 5 + CHUNK]
            for tap in range(1, 4):
                summed = summed + conv_ref[tap : tap + 1, :] * window[5 + tap : 5 + tap + CHUNK]
            active = silu(summed)
            query = unit_rows(active[:, :DK]) * DK ** (-0.5)
            key = unit_rows(active[:, DK : 2 * DK])
            rate = rate_scr[pl.ds(at, CHUNK), :]
            shifted = rate + rate_par_ref[0:1, :]
            soft = jnp.maximum(shifted, 0.0) + jnp.log1p(jnp.exp(-jnp.abs(shifted)))
            decay = -rate_par_ref[1:2, :] * soft
            beta_all = 1.0 / (1.0 + jnp.exp(-rate))
            total = jnp.dot(lower, decay, preferred_element_type=f32, precision=highest)
            total_t = total.T
            key_low = key.astype(bf16)
            gram = mm_t(key_low, key_low)
            raw_scores = mm_t(query, key_low)
            for h in range(HEADS):
                cum = total[:, HEADS + h : HEADS + h + 1]
                cum_row = total_t[HEADS + h : HEADS + h + 1, :]
                beta = beta_all[:, h : h + 1]
                causal = jnp.exp(jnp.where(row >= col, cum - cum_row, -1e30))
                grown = jnp.exp(cum)
                last = cum[CHUNK - 1 : CHUNK, :]
                value = active[:, 2 * DK + h * DV : 2 * DK + (h + 1) * DV]
                units.append(
                    dict(
                        at=at,
                        h=h,
                        low=jnp.where(row > col, beta * gram * causal, 0.0),
                        right=jnp.concatenate([beta * key * grown, beta * value], axis=1).astype(bf16),
                        scores=(raw_scores * causal).astype(bf16),
                        read=(query * grown).astype(bf16),
                        faded=(key * jnp.exp(last - cum)).T.astype(bf16),
                        fade=jnp.exp(last),
                    )
                )
        inverses = [
            eye - jnp.where((row // 2 == col // 2), unit["low"], 0.0) for unit in units
        ]
        size = 2
        while size < CHUNK:
            off = (row // (2 * size) == col // (2 * size)) & (row // size != col // size)
            lows = [x.astype(bf16) for x in inverses]
            firsts = [mm(jnp.where(off, unit["low"], 0.0), x) for unit, x in zip(units, lows)]
            inverses = [x - mm(x_low, y) for x, x_low, y in zip(inverses, lows, firsts)]
            size *= 2
        solved = [mm(x, unit["right"]) for unit, x in zip(units, inverses)]
        for unit, done in zip(units, solved):
            h = unit["h"]
            state = summary_ref[h]
            stacked = jnp.concatenate([done[:, :DK].astype(bf16), unit["read"]], axis=0)
            applied = mm(stacked, state)
            fresh = jnp.concatenate([-applied[:CHUNK, :DK], done[:, DK:] - applied[:CHUNK, DK:]], axis=1)
            fresh = fresh.astype(bf16)
            out = applied[CHUNK:] + mm(unit["scores"], fresh)
            summary_ref[h] = unit["fade"] * state + mm(unit["faded"], fresh)
            reader_ref[h, pl.ds(unit["at"], CHUNK), :] = out[:, :DK].astype(bf16)
            local_ref[h, pl.ds(unit["at"], CHUNK), :] = out[:, DK:]
        return 0

    lax.fori_loop(0, steps // pair, chunk_step, 0)
    for h in range(HEADS):
        packed_ref[h, :, :DK] = (summary_ref[h, :, :DK] - eye).astype(bf16)
        packed_ref[h, :, DK:] = summary_ref[h, :, DK:].astype(bf16)


def run_delta(segment, halo, weight, conv, rate_par):
    rows = segment.shape[0]
    return pl.pallas_call(
        delta_kernel,
        out_shape=(
            jax.ShapeDtypeStruct((rows, HEADS * DV), bf16),
            jax.ShapeDtypeStruct((HEADS, rows, DK), bf16),
            jax.ShapeDtypeStruct((HEADS, rows, DV), f32),
            jax.ShapeDtypeStruct((HEADS, DK, DK + DV), f32),
            jax.ShapeDtypeStruct((HEADS, DK, DK + DV), bf16),
        ),
        in_specs=[VMEM] * 5,
        out_specs=(VMEM,) * 5,
        scratch_shapes=[
            pltpu.VMEM((rows + 8, conv.shape[1]), f32),
            pltpu.VMEM((rows, 128), f32),
        ],
        compiler_params=pltpu.CompilerParams(vmem_limit_bytes=GRANT),
        name="delta",
        cost_estimate=pl.CostEstimate(flops=12 * 10**9, bytes_accessed=12 * 10**6, transcendentals=0),
    )(segment, halo, weight, conv, rate_par)


def compose(state, packed):
    moved = state + mm(packed[:, :DK], state)
    return moved, packed[:, DK:].astype(f32)


def row_kernel(place_ref, all_ref, prefix_ref, total_ref):
    place = place_ref[0]
    count = all_ref.shape[0]
    eye = (square_iota(DK, 0) == square_iota(DK, 1)).astype(f32)
    zero = jnp.zeros((DK, DV), f32)
    states = [jnp.concatenate([eye, zero], axis=1) for _ in range(HEADS)]
    for j in range(count):
        for h in range(HEADS):
            state = states[h]

            @pl.when(place == j)
            def _(state=state, h=h):
                prefix_ref[h] = state

            moved, added = compose(state, all_ref[j, h])
            states[h] = jnp.concatenate([moved[:, :DK], moved[:, DK:] + added], axis=1)
    for h in range(HEADS):
        total_ref[h, :, :DK] = (states[h][:, :DK] - eye).astype(bf16)
        total_ref[h, :, DK:] = states[h][:, DK:].astype(bf16)


def run_row(place, gathered):
    return pl.pallas_call(
        row_kernel,
        out_shape=(
            jax.ShapeDtypeStruct(gathered.shape[1:], f32),
            jax.ShapeDtypeStruct(gathered.shape[1:], bf16),
        ),
        in_specs=[SMEM, VMEM],
        out_specs=(VMEM, VMEM),
        compiler_params=pltpu.CompilerParams(vmem_limit_bytes=GRANT),
        name="row",
    )(place, gathered)


def finish_kernel(
    place_ref, rows_ref, start_ref, prefix_ref, summary_ref, reader_ref, local_ref, gate_ref, gain_ref, weight_ref,
    out_ref, final_ref,
):
    place = place_ref[0]
    count = rows_ref.shape[0]
    eye = (square_iota(DK, 0) == square_iota(DK, 1)).astype(f32)
    entering = []
    for h in range(HEADS):
        state = start_ref[h]
        for j in range(count - 1):
            moved, added = compose(state, rows_ref[j, h])
            state = jnp.where(place > j, moved + added, state)
        state = state + mm(prefix_ref[h, :, :DK] - eye, state) + prefix_ref[h, :, DK:]
        final_ref[h] = state + mm(summary_ref[h, :, :DK] - eye, state) + summary_ref[h, :, DK:]
        entering.append(state.astype(bf16))

    def tile(i, _):
        at = pl.ds(pl.multiple_of(i * CHUNK, CHUNK), CHUNK)
        parts = []
        for h in range(HEADS):
            mixed = mm(reader_ref[h, at, :], entering[h]) + local_ref[h, at, :]
            gate = gate_ref[at, h * DV : (h + 1) * DV].astype(f32)
            parts.append((rms_scale(mixed, gain_ref[...]) * silu(gate)).astype(bf16))
        gated = jnp.concatenate(parts, axis=1)
        out_ref[at, :] = jnp.dot(gated, weight_ref[...], preferred_element_type=f32).astype(bf16)
        return 0

    lax.fori_loop(0, reader_ref.shape[1] // CHUNK, tile, 0)


def run_finish(place, rows, start, prefix, summary, reader, local, gate, gain, weight):
    return pl.pallas_call(
        finish_kernel,
        out_shape=(
            jax.ShapeDtypeStruct((gate.shape[0], weight.shape[1]), bf16),
            jax.ShapeDtypeStruct(start.shape, f32),
        ),
        in_specs=[SMEM] + [VMEM] * 9,
        out_specs=(VMEM, VMEM),
        compiler_params=pltpu.CompilerParams(vmem_limit_bytes=GRANT),
        name="finish",
    )(place, rows, start, prefix, summary, reader, local, gate, gain, weight)


def dispatch_kernel(own_ref, mixed_ref, gain_ref, pick_ref, hidden_ref, out_ref):
    hidden = own_ref[...].astype(f32) + mixed_ref[...].astype(f32)
    hidden_ref[...] = hidden
    post = rms_scale(hidden, gain_ref[...]).astype(bf16)
    half = post.shape[1] // 2
    stacked = jnp.concatenate([post[:, :half], post[:, half:]], axis=0)
    out_ref[...] = jnp.dot(pick_ref[...], stacked, preferred_element_type=f32).astype(bf16)


def run_dispatch(own, mixed, gain, pick):
    return pl.pallas_call(
        dispatch_kernel,
        out_shape=(
            jax.ShapeDtypeStruct(own.shape, f32),
            jax.ShapeDtypeStruct((pick.shape[0], own.shape[1] // 2), bf16),
        ),
        in_specs=[VMEM] * 4,
        out_specs=(VMEM, VMEM),
        compiler_params=pltpu.CompilerParams(vmem_limit_bytes=GRANT),
        name="dispatch",
    )(own, mixed, gain, pick)


def expert_kernel(rows_ref, up_ref, down_ref, out_ref):
    count, _, half = rows_ref.shape

    def hidden_of(gate_up):
        return (silu(gate_up[:, :FFE]) * gate_up[:, FFE:]).astype(bf16)

    group = 8

    def step(i, _):
        some = pl.ds(i * group, group)
        left = rows_ref[some, 0:16, :].reshape(group * 16, half)
        right = rows_ref[some, 16:32, :].reshape(group * 16, half)
        gate_up = jnp.dot(left, up_ref[:half, :], preferred_element_type=f32) + jnp.dot(
            right, up_ref[half:, :], preferred_element_type=f32
        )
        done = jnp.dot(hidden_of(gate_up), down_ref[...], preferred_element_type=f32).astype(bf16)
        out_ref[some, 0:16, :] = done[:, :half].reshape(group, 16, half)
        out_ref[some, 16:32, :] = done[:, half:].reshape(group, 16, half)
        return 0

    lax.fori_loop(0, count // group, step, 0)
    tail = rows_ref[:, 32:40, :].reshape(count * 8, half)
    first = jnp.dot(tail, up_ref[:half, :], preferred_element_type=f32)
    second = jnp.dot(tail, up_ref[half:, :], preferred_element_type=f32)
    turned = count * 8 - 4
    gate_up = first + pltpu.roll(second, turned, 0)
    done = jnp.dot(hidden_of(gate_up), down_ref[...], preferred_element_type=f32)
    upper = lax.broadcasted_iota(jnp.int32, (count * 8, half), 0) % 8 < 4
    packed = jnp.where(upper, done[:, :half], pltpu.roll(done[:, half:], 4, 0)).astype(bf16)
    out_ref[:, 32:40, :] = packed.reshape(count, 8, half)


def run_expert(rows, up, down):
    return pl.pallas_call(
        expert_kernel,
        out_shape=jax.ShapeDtypeStruct(rows.shape, bf16),
        in_specs=[VMEM] * 3,
        out_specs=VMEM,
        compiler_params=pltpu.CompilerParams(vmem_limit_bytes=GRANT),
        name="expert",
    )(rows, up, down)


def combine_kernel(hidden_ref, back_ref, high_ref, low_ref, out_ref):
    rows = hidden_ref.shape[0]
    half = back_ref.shape[1]
    back = back_ref[...]
    routed = jnp.dot(high_ref[...], back, preferred_element_type=f32) + jnp.dot(
        low_ref[...], back, preferred_element_type=f32
    )
    out_ref[:, :half] = hidden_ref[:, :half] + routed[:rows]
    out_ref[:, half:] = hidden_ref[:, half:] + routed[rows:]


def run_combine(hidden, back, high, low):
    return pl.pallas_call(
        combine_kernel,
        out_shape=jax.ShapeDtypeStruct(hidden.shape, f32),
        in_specs=[VMEM] * 4,
        out_specs=VMEM,
        compiler_params=pltpu.CompilerParams(vmem_limit_bytes=GRANT),
        name="combine",
    )(hidden, back, high, low)


def slot_rows(ids, experts):
    rows = ids.shape[0]
    choice = ids[:, :, None] == jnp.arange(experts, dtype=jnp.int32)
    named = jnp.any(choice, axis=1).astype(bf16)
    before = jnp.tril(jnp.ones((rows, rows), bf16), -1)
    ranks = jnp.dot(before, named, preferred_element_type=f32)
    slots = jnp.sum(jnp.where(choice, ranks[:, None, :], 0.0), axis=2).astype(jnp.int32)
    early = slots < 16
    left = ids * 40 + jnp.where(early, slots, slots + 16)
    right = ids * 40 + jnp.where(early, slots + 16, slots + 20)
    return jnp.concatenate([left, right], axis=0)


def body(
    tokens,
    input_gain,
    mixer_weight,
    rate_weight,
    conv_kernel,
    decay_scale,
    decay_bias,
    value_gain,
    output_weight,
    start_state,
    post_gain,
    expert_gateup,
    expert_down,
    route_ids,
    route_weights,
):
    own = tokens[0]
    model_width = own.shape[1]
    experts = lax.axis_size(EXP)
    normed = rms_scale(own, input_gain).astype(bf16)
    segment = lax.all_gather(normed, CTX, axis=0, tiled=True)
    last_rows = lax.ppermute(normed[-8:], EXP, [(i, i + 1) for i in range(experts - 1)])
    halo = lax.all_gather(last_rows, CTX, axis=0)[-1]
    weight = jnp.concatenate(
        [
            mixer_weight,
            rate_weight.reshape(model_width, -1),
            jnp.zeros((model_width, 128 - 2 * HEADS), bf16),
        ],
        axis=1,
    )
    room = 128 - 2 * HEADS
    rate_par = jnp.stack(
        [
            jnp.concatenate([jnp.zeros(HEADS, f32), decay_bias, jnp.zeros(room, f32)]),
            jnp.concatenate([jnp.zeros(HEADS, f32), decay_scale, jnp.zeros(room, f32)]),
        ]
    )
    gate, reader, local, summary, packed = run_delta(
        segment, halo, weight, conv_kernel[:, 0], rate_par
    )
    depth = lax.axis_size("z")
    gathered = lax.all_to_all(
        jnp.broadcast_to(packed[None], (depth,) + packed.shape), "z", 0, 0, tiled=True
    )
    prefix, total = run_row(lax.axis_index("z").reshape(1), gathered)
    rows = lax.all_gather(total, "x", axis=0)
    partial, final_state = run_finish(
        lax.axis_index("x").reshape(1), rows, start_state, prefix, summary, reader, local, gate,
        value_gain.reshape(1, -1), output_weight,
    )
    mixed = lax.psum_scatter(partial, CTX, scatter_dimension=0, tiled=True)

    places = slot_rows(route_ids[0], experts)
    count = experts * 40
    hits = places[:, :, None] == jnp.arange(count, dtype=jnp.int32)
    pick = jnp.any(
        places.T[:, None, :] == jnp.arange(count, dtype=jnp.int32)[None, :, None], axis=0
    ).astype(bf16)
    doubled = jnp.concatenate([route_weights[0], route_weights[0]], axis=0)
    share = jnp.sum(jnp.where(hits, doubled[:, :, None], 0.0), axis=1)
    high = share.astype(bf16)
    low = (share - high.astype(f32)).astype(bf16)

    hidden, outgoing = run_dispatch(own, mixed, post_gain.reshape(1, -1), pick)
    half = model_width // 2
    arrived = lax.all_to_all(outgoing.reshape(experts, 40, half), EXP, 0, 0, tiled=True)
    made = run_expert(arrived, expert_gateup[0], expert_down[0])
    back = lax.all_to_all(made, EXP, 0, 0, tiled=True)
    layer_out = run_combine(hidden, back.reshape(count, half), high, low)
    return (layer_out[None], final_state[None])


def solution(mesh):
    fine = Mesh(mesh.devices.reshape(4, 2, 4, 8), CTX + EXP)
    in_specs = (
        P(EXP, CTX, None),
        P(),
        P(None, CTX),
        P(None, CTX, None),
        P(None, CTX, None),
        P(CTX),
        P(CTX),
        P(),
        P(CTX, None),
        P(CTX, None, None),
        P(),
        P(EXP, None, None),
        P(EXP, None, None),
        P(EXP, CTX, None),
        P(EXP, CTX, None),
    )
    out_specs = (P(EXP, CTX, None), P(EXP, CTX, None, None))
    return jax.shard_map(body, mesh=fine, in_specs=in_specs, out_specs=out_specs, check_vma=False)
```

time: 757 us -> 344 us (0.45)
  starting transfers between devices: 184 us -> 18.7 us
  matrix products: 130 us -> 0.2 us
  waiting for transfers between devices: 256 us -> 131 us
  Pallas kernels: 0 us -> 59 us
  local copies, waits for them, and re-layouts: 49.8 us -> 7.57 us
  blocking collectives: 83.4 us -> 98.8 us
  other arithmetic: 27.2 us -> 13.4 us
    ppermute x32 -> x1, starting transfers between devices: 178 us -> 3.81 us  [body(): lax.ppermute(normed[-8:], EXP, [(i, i + 1) for i in range(experts - 1)])]
    dot_general x117 -> x1, matrix products: 130 us -> 0.2 us  [slot_rows(): ranks = jnp.dot(before, named, preferred_element_type=f32)]
    ppermute x32 -> x1, waiting for transfers between devices: 82.6 us -> 0.01 us  [body(): lax.ppermute(normed[-8:], EXP, [(i, i + 1) for i in range(experts - 1)])]
    pallas_call x0 -> x6, Pallas kernels: none -> 59 us  [the longest x1 24.5 us: run_delta(): pl.pallas_call(delta_kernel, out_shape=(jax.ShapeDtypeStruct((rows, HEADS...]
    reduce_scatter x1, waiting for transfers between devices: 66.7 us -> 30.2 us  [body(): mixed = lax.psum_scatter(partial, CTX, scatter_dimension=0, tiled=True)]
    all_gather x0 -> x2, blocking collectives: none -> 27.9 us  [the longest x1 14.7 us: body(): rows = lax.all_gather(total, 'x', axis=0)]
    all_gather x1, waiting for transfers between devices: 33.1 us -> 10.3 us  [body(): segment = lax.all_gather(normed, CTX, axis=0, tiled=True)]
    all_to_all x1 -> x2, waiting for transfers between devices: 74 us -> 90.9 us  [the longest x1 61.8 us: body(): back = lax.all_to_all(made, EXP, 0, 0, tiled=True)]
  transfers between devices with their start and end apart: 35 -> 5, of which waited for: 34 -> 4; matrix products, arithmetic and copies ran while one was open for 3% -> 4% of each run, Pallas kernels for 0% -> 0%
where the time goes in v1:
time: 344 us; the launch traced here: 343 us
  waiting for transfers between devices  131 us (38%)
  blocking collectives  98.8 us (29%)
  Pallas kernels  59 us (17%)
  starting transfers between devices  18.7 us (5%)
  between operations  14.2 us (4%)
  other arithmetic  13.4 us (4%)
  local copies, waits for them, and re-layouts  7.57 us (2%)
    all_to_all x1, blocking collectives, body(): lax.all_to_all(outgoing.reshape(experts, 40, half), EXP, 0, 0, tiled=True)  70.9 us
    all_to_all x1, waiting for transfers between devices, body(): back = lax.all_to_all(made, EXP, 0, 0, tiled=True)  61.8 us
    reduce_scatter x1, waiting for transfers between devices, body(): mixed = lax.psum_scatter(partial, CTX, scatter_dimension=0, tiled=True)  30.2 us
    all_to_all x1, waiting for transfers between devices, body(): lax.all_to_all(jnp.broadcast_to(packed[None], (depth,) + packed.shape), '...  29.1 us
    pallas_call x1, Pallas kernels, run_delta(): pl.pallas_call(delta_kernel, out_shape=(jax.ShapeDtypeStruct((rows, HEADS...  24.5 us
    all_gather x1, blocking collectives, body(): rows = lax.all_gather(total, 'x', axis=0)  14.7 us
    all_gather x1, blocking collectives, body(): halo = lax.all_gather(last_rows, CTX, axis=0)[-1]  13.2 us
    pallas_call x1, Pallas kernels, run_expert(): pl.pallas_call(expert_kernel, out_shape=jax.ShapeDtypeStruct(rows.shape,...  11.5 us
  transfers between devices with their start and end apart: 5, of which 4 were waited for; matrix products, arithmetic and copies ran while one was open for 4% of the time, Pallas kernels for 0%

profile of v1, /device:TPU:24, one launch (start us, length us, event | category | flops | bytes accessed | tf_op | source)
XLA Modules:
  0.0 343.3 jit_solution(5236530405454612094)
XLA Ops:
  7.2 0.0 all-gather.4.cloned.1.call-start
  7.2 1.2 fusion.1
  8.4 2.0 fusion.3
  10.5 0.0 all-gather.4.cloned.1.call-update
  10.5 0.8 slice.9
  11.3 3.8 %collective-permute-start = (bf16[8,2048]{1,0:T(8,128)(2,1)S(1)}, bf16[8,2048]{1,0:T(8,128)(2,1)S(1)}, u32[]{:S(2)}, u32[]{:S(2)}) collective-permute-start(bf16[8,2048]{1,0:T(8,128)(2,1)S(1)} %slice.9), channel_id=1, source_target_pairs={{0,1},{1,2},{2,3},{3,4},{4,5},{5,6},{6,7},{7,8},{8,9},{9,10},{10,1... | collective-permute-start | bytes 98312 | tf_op jit(solution)/shard_map/ppermute | solution.py:393
  15.1 1.0 copy.27
  16.1 0.1 pad.14.clone
  16.2 0.7 fusion.13
  17.0 0.0 copy-start.3
  17.0 4.5 %maximum_maximum_fusion.weight_ref = bf16[2048,896]{1,0:T(8,128)(2,1)} fusion(bf16[2048,4]{1,0:T(8,128)(2,1)S(1)} %bitcast.35, bf16[2048,768]{1,0:T(8,128)(2,1)} %param.17, bf16[896]{0:T(1024)(128)(2,1)S(1)} %pad.14.clone), kind=kLoop, calls=%fused_computation.4 | loop fusion | flops 11010048 | bytes 6833920 | tf_op jit(solution)/shard_map/concatenate | solution.py:395
  21.4 0.5 pad_maximum_fusion.1.rate_par_ref
  22.0 0.0 copy-done.3
  22.0 0.6 copy.30
  22.6 0.0 collective-permute-done
  22.6 13.2 %all-gather = bf16[64,2048]{1,0:T(8,128)(2,1)S(1)} all-gather(bf16[8,2048]{1,0:T(8,128)(2,1)S(1)} %collective-permute-done), channel_id=2, replica_groups=mesh['y'=4,'core'=2,'x'=4,'z'=8] {'y','core'}, dimensions={0}, use_global_device_ids=true | all-gather | bytes 294912 | tf_op jit(solution)/shard_map/all_gather | solution.py:394
  35.8 0.6 slice.10.halo_ref
  36.4 10.3 %all-gather.4.cloned.1.call-done.seg_ref = bf16[1024,2048]{1,0:T(8,128)(2,1)} async-done(((bf16[128,2048]{1,0:T(8,128)(2,1)}), bf16[1024,2048]{1,0:T(8,128)(2,1)}) %all-gather.4.cloned.1.call-update) | async-done | bytes 4194320 | tf_op jit(solution)/shard_map/all_gather | solution.py:392
  46.7 24.5 %delta.1 = (bf16[1024,256]{1,0:T(8,128)(2,1)}, bf16[2,1024,128]{2,1,0:T(8,128)(2,1)}, f32[2,1024,128]{2,1,0:T(8,128)}, f32[2,128,256]{2,1,0:T(8,128)}, bf16[2,128,256]{2,1,0:T(8,128)(2,1)}) custom-call(bf16[1024,2048]{1,0:T(8,128)(2,1)} %all-gather.4.cloned.1.call-done.seg_ref, bf16[8,2048]{1,0:T(8,128)(2,1)} %slice.10.halo_ref, ...), custom_call_target="tpu_custom_call" | custom-call | flops 12000000000 | bytes 12000000 | tf_op jit(solution)/shard_map/delta/pallas_call | solution.py:164
  71.2 2.0 broadcast_in_dim.56
  73.2 7.2 %all-to-all-start = ((bf16[8,2,128,256]{3,2,1,0:T(8,128)(2,1)}), bf16[8,2,128,256]{3,2,1,0:T(8,128)(2,1)S(1)}, u32[]{:S(2)}, u32[]{:S(2)}) async-start(bf16[8,2,128,256]{3,2,1,0:T(8,128)(2,1)} %broadcast_in_dim.56), calls=%async_computation | async-start | bytes 2097152 | tf_op jit(solution)/shard_map/all_to_all | solution.py:414
  80.4 0.0 reduce-scatter.2.cloned.1.call-start
  80.5 29.1 %all-to-all-done.all_ref = bf16[8,2,128,256]{3,2,1,0:T(8,128)(2,1)S(1)} async-done(((bf16[8,2,128,256]{3,2,1,0:T(8,128)(2,1)}), bf16[8,2,128,256]{3,2,1,0:T(8,128)(2,1)S(1)}, u32[]{:S(2)}, u32[]{:S(2)}) %all-to-all-start) | async-done | bytes 1048608 | tf_op jit(solution)/shard_map/all_to_all | solution.py:414
  109.6 0.0 copy-start.1
  109.6 1.0 copy-done.1
  110.6 4.5 %row.1 = (f32[2,128,256]{2,1,0:T(8,128)}, bf16[2,128,256]{2,1,0:T(8,128)(2,1)}) custom-call(s32[1]{0:T(128)} %bitcast.2.place_ref, bf16[8,2,128,256]{3,2,1,0:T(8,128)(2,1)} %copy-done.1), custom_call_target="tpu_custom_call" | custom-call | tf_op jit(solution)/shard_map/row/pallas_call | solution.py:212
  115.1 14.7 %all-gather.1 = bf16[8,128,256]{2,1,0:T(8,128)(2,1)} all-gather(bf16[2,128,256]{2,1,0:T(8,128)(2,1)} %get-tuple-element.14), channel_id=3, replica_groups=mesh['y'=4,'core'=2,'x'=4,'z'=8] {'x'}, dimensions={0}, use_global_device_ids=true | all-gather | bytes 655360 | tf_op jit(solution)/shard_map/all_gather | solution.py:418
  129.8 0.0 copy-start.2
  129.8 9.5 %finish.1 = (bf16[1024,2048]{1,0:T(8,128)(2,1)}, f32[2,128,128]{2,1,0:T(8,128)}) custom-call(s32[1]{0:T(128)} %bitcast.1.place_ref, bf16[4,2,128,256]{3,2,1,0:T(8,128)(2,1)} %bitcast.33, f32[2,128,128]{2,1,0:T(8,128)} %start_ref.1, f32[2,128,256]{2,1,0:T(8,128)} %get-tuple-element.15.prefix_ref, f32[2,128,256]{2,1,0:T(8,128)} %get-tuple-element.16.summary_ref, ...), custom_call_target="tpu_custom_call" | custom-call | tf_op jit(solution)/shard_map/finish/pallas_call | solution.py:257
  139.3 0.0 reduce-scatter.2.cloned.1.call-update
  139.4 0.0 copy-done.2
  139.4 0.2 fusion.6
  139.7 1.5 fusion
  141.2 1.0 convert_element_type.25.pick_ref
  142.2 30.2 %reduce-scatter.2.cloned.1.call-done.mixed_ref = bf16[128,2048]{1,0:T(8,128)(2,1)} async-done(((bf16[1024,2048]{1,0:T(8,128)(2,1)}), bf16[128,2048]{1,0:T(8,128)(2,1)}) %reduce-scatter.2.cloned.1.call-update) | async-done | bytes 524304 | tf_op jit(solution)/shard_map/reduce_scatter | solution.py:423
  172.4 4.0 %dispatch.1 = (f32[128,2048]{1,0:T(8,128)}, bf16[1280,1024]{1,0:T(8,128)(2,1)}) custom-call(bf16[128,2048]{1,0:T(8,128)(2,1)} %bitcast.30, bf16[128,2048]{1,0:T(8,128)(2,1)} %reduce-scatter.2.cloned.1.call-done.mixed_ref, f32[1,2048]{1,0:T(1,128)} %bitcast.39, bf16[1280,256]{1,0:T(8,128)(2,1)} %convert_element_type.25.pick_ref), custom_call_target="tpu_custom_call" | custom-call | tf_op jit(solution)/shard_map/dispatch/pallas_call | solution.py:280
  176.4 70.9 %all_to_all.15.rows_ref = bf16[32,40,1024]{2,1,0:T(8,128)(2,1)} all-to-all(bf16[32,40,1024]{2,1,0:T(8,128)(2,1)} %bitcast.32), channel_id=1, replica_groups=mesh['y'=4,'core'=2,'x'=4,'z'=8] {'x','z'}, dimensions={0} | all-to-all | bytes 5242880 | tf_op jit(solution)/shard_map/all_to_all | solution.py:438
  247.3 11.5 %expert.1 = bf16[32,40,1024]{2,1,0:T(8,128)(2,1)} custom-call(bf16[32,40,1024]{2,1,0:T(8,128)(2,1)} %all_to_all.15.rows_ref, bf16[2048,1024]{1,0:T(8,128)(2,1)} %bitcast.31, bf16[512,2048]{1,0:T(8,128)(2,1)} %bitcast.34), custom_call_target="tpu_custom_call" | custom-call | tf_op jit(solution)/shard_map/expert/pallas_call | solution.py:326
  258.8 0.0 copy-start.4
  258.8 7.5 %all-to-all-start.2 = ((bf16[32,40,1024]{2,1,0:T(8,128)(2,1)}), bf16[32,40,1024]{2,1,0:T(8,128)(2,1)S(1)}, u32[]{:S(2)}, u32[]{:S(2)}) async-start(bf16[32,40,1024]{2,1,0:T(8,128)(2,1)} %expert.1), calls=%async_computation.3 | async-start | bytes 5242880 | tf_op jit(solution)/shard_map/all_to_all | solution.py:440
  266.4 0.0 copy-done.4
  266.4 0.7 select_reduce_fusion
  267.1 1.2 subtract_convert_fusion
  268.3 61.8 %all-to-all-done.2 = bf16[32,40,1024]{2,1,0:T(8,128)(2,1)S(1)} async-done(((bf16[32,40,1024]{2,1,0:T(8,128)(2,1)}), bf16[32,40,1024]{2,1,0:T(8,128)(2,1)S(1)}, u32[]{:S(2)}, u32[]{:S(2)}) %all-to-all-start.2) | async-done | bytes 2621472 | tf_op jit(solution)/shard_map/all_to_all | solution.py:440
  330.1 0.0 copy-start
  330.1 1.5 copy-done
  331.6 4.9 %combine.1 = f32[128,2048]{1,0:T(8,128)} custom-call(f32[128,2048]{1,0:T(8,128)} %get-tuple-element.21.hidden_ref, bf16[1280,1024]{1,0:T(8,128)(2,1)} %bitcast.29, bf16[256,1280]{1,0:T(8,128)(2,1)} %get-tuple-element.25.high_ref, bf16[256,1280]{1,0:T(8,128)(2,1)} %get-tuple-element.24.low_ref), custom_call_target="tpu_custom_call" | custom-call | tf_op jit(solution)/shard_map/combine/pallas_call | solution.py:348
  (10 shorter events, 0.1 us)
Async XLA Ops:
  7.2 39.5 %all-gather.4.cloned.1.call-start = ((), (), s32[]{:S(2)}) async-start(), calls=%async_computation.4 | async-start | bytes 4718592 | tf_op jit(solution)/shard_map/all_gather | solution.py:392
  11.3 11.3 %collective-permute-start = (bf16[8,2048]{1,0:T(8,128)(2,1)S(1)}, bf16[8,2048]{1,0:T(8,128)(2,1)S(1)}, u32[]{:S(2)}, u32[]{:S(2)}) collective-permute-start(bf16[8,2048]{1,0:T(8,128)(2,1)S(1)} %slice.9), channel_id=1, source_target_pairs={{0,1},{1,2},{2,3},{3,4},{4,5},{5,6},{6,7},{7,8},{8,9},{9,10},{10,1... | collective-permute-start | bytes 98312 | tf_op jit(solution)/shard_map/ppermute | solution.py:393
  17.0 5.0 %copy-start.3 = (f32[4,1,512]{2,1,0:T(1,128)S(1)}, f32[4,1,512]{2,1,0:T(1,128)}, u32[]{:S(2)}) copy-start(f32[4,1,512]{2,1,0:T(1,128)} %param.19) | copy-start | bytes 24580
  73.2 36.4 %all-to-all-start = ((bf16[8,2,128,256]{3,2,1,0:T(8,128)(2,1)}), bf16[8,2,128,256]{3,2,1,0:T(8,128)(2,1)S(1)}, u32[]{:S(2)}, u32[]{:S(2)}) async-start(bf16[8,2,128,256]{3,2,1,0:T(8,128)(2,1)} %broadcast_in_dim.56), calls=%async_computation | async-start | bytes 2097152 | tf_op jit(solution)/shard_map/all_to_all | solution.py:414
  80.4 92.0 %reduce-scatter.2.cloned.1.call-start = ((), (), s32[]{:S(2)}) async-start(), calls=%async_computation.5 | async-start | bytes 4718592 | tf_op jit(solution)/shard_map/reduce_scatter | solution.py:423
  109.6 1.0 copy-start.1
  129.8 9.6 %copy-start.2 = (s32[1,128,4]{1,2,0:T(4,128)S(1)}, s32[1,128,4]{1,2,0:T(4,128)}, u32[]{:S(2)}) copy-start(s32[1,128,4]{1,2,0:T(4,128)} %param.28) | copy-start | bytes 6148
  258.8 7.5 %copy-start.4 = (f32[1,128,4]{1,2,0:T(4,128)S(1)}, f32[1,128,4]{1,2,0:T(4,128)}, u32[]{:S(2)}) copy-start(f32[1,128,4]{1,2,0:T(4,128)} %param.29) | copy-start | bytes 6148
  258.8 71.2 %all-to-all-start.2 = ((bf16[32,40,1024]{2,1,0:T(8,128)(2,1)}), bf16[32,40,1024]{2,1,0:T(8,128)(2,1)S(1)}, u32[]{:S(2)}, u32[]{:S(2)}) async-start(bf16[32,40,1024]{2,1,0:T(8,128)(2,1)} %expert.1), calls=%async_computation.3 | async-start | bytes 5242880 | tf_op jit(solution)/shard_map/all_to_all | solution.py:440
  330.1 1.5 copy-start
Sparse Core Ops, SparseCore 0:
  10.6 35.9 all-gather.3
  139.5 32.8 reduce-scatter.1

commit v2 on v1

--- a/solution.py
+++ b/solution.py
@@ -14,6 +14,7 @@
 HEADS = 2
 ROUTES = 4
 CHUNK = 128
+TILE = 512
 EPSILON = 1e-06
 CTX = ("y", "core")
 EXP = ("x", "z")
@@ -22,7 +23,7 @@
 highest = lax.Precision.HIGHEST
 VMEM = pl.BlockSpec(memory_space=pltpu.VMEM)
 SMEM = pl.BlockSpec(memory_space=pltpu.SMEM)
-GRANT = 56 * 1024 * 1024
+GRANT = 24 * 1024 * 1024
 
 
 def mm(a, b):
@@ -69,14 +70,14 @@
     rows_scr[0:8, :] = project(halo_ref[...])[:, :width].astype(f32)
 
     def project_step(i, _):
-        at = pl.multiple_of(i * CHUNK, CHUNK)
-        made = project(seg_ref[pl.ds(at, CHUNK), :])
-        rows_scr[pl.ds(pl.multiple_of(at + 8, 8), CHUNK), :] = made[:, :width].astype(f32)
-        gate_ref[pl.ds(at, CHUNK), :] = made[:, width : width + HEADS * DV]
-        rate_scr[pl.ds(at, CHUNK), :] = made[:, width + HEADS * DV :].astype(f32)
+        at = pl.multiple_of(i * TILE, TILE)
+        made = project(seg_ref[pl.ds(at, TILE), :])
+        rows_scr[pl.ds(pl.multiple_of(at + 8, 8), TILE), :] = made[:, :width].astype(f32)
+        gate_ref[pl.ds(at, TILE), :] = made[:, width : width + HEADS * DV]
+        rate_scr[pl.ds(at, TILE), :] = made[:, width + HEADS * DV :].astype(f32)
         return 0
 
-    lax.fori_loop(0, steps, project_step, 0)
+    lax.fori_loop(0, seg_rows // TILE, project_step, 0)
 
     row = square_iota(CHUNK, 0)
     col = square_iota(CHUNK, 1)
@@ -86,7 +87,7 @@
         summary_ref[h, :, :DK] = eye
         summary_ref[h, :, DK:] = jnp.zeros((DK, DV), f32)
 
-    pair = 2
+    pair = 8
 
     def chunk_step(i, _):
         units = []
@@ -155,7 +156,9 @@
 
     lax.fori_loop(0, steps // pair, chunk_step, 0)
     for h in range(HEADS):
-        packed_ref[h, :, :DK] = (summary_ref[h, :, :DK] - eye).astype(bf16)
+        change = summary_ref[h, :, :DK] - eye
+        summary_ref[h, :, :DK] = change
+        packed_ref[h, :, :DK] = change.astype(bf16)
         packed_ref[h, :, DK:] = summary_ref[h, :, DK:].astype(bf16)
 
 
@@ -182,65 +185,85 @@
     )(segment, halo, weight, conv, rate_par)
 
 
-def compose(state, packed):
-    moved = state + mm(packed[:, :DK], state)
-    return moved, packed[:, DK:].astype(f32)
-
-
-def row_kernel(place_ref, all_ref, prefix_ref, total_ref):
-    place = place_ref[0]
-    count = all_ref.shape[0]
-    eye = (square_iota(DK, 0) == square_iota(DK, 1)).astype(f32)
-    zero = jnp.zeros((DK, DV), f32)
-    states = [jnp.concatenate([eye, zero], axis=1) for _ in range(HEADS)]
-    for j in range(count):
+def then(first, second):
+    return first + mm(second[:, :DK], first) + second.astype(f32)
+
+
+def apply(change, state):
+    return state + mm(change[:, :DK], state) + change[:, DK:].astype(f32)
+
+
+def couple_kernel(place_ref, own_ref, other_ref, both_ref):
+    odd = place_ref[0] % 2 == 1
+    for h in range(HEADS):
+        own = own_ref[h].astype(f32)
+        other = other_ref[h].astype(f32)
+        both_ref[h] = then(jnp.where(odd, other, own), jnp.where(odd, own, other)).astype(bf16)
+
+
+def run_couple(place, own, other):
+    return pl.pallas_call(
+        couple_kernel,
+        out_shape=jax.ShapeDtypeStruct(own.shape, bf16),
+        in_specs=[SMEM, VMEM, VMEM],
+        out_specs=VMEM,
+        compiler_params=pltpu.CompilerParams(vmem_limit_bytes=8 * 1024 * 1024),
+        name="couple",
+    )(place, own, other)
+
+
+def row_kernel(place_ref, own_ref, back1_ref, back2_ref, back3_ref, other_ref, prefix_ref, total_ref, all_scr):
+    odd = place_ref[0] % 2 == 1
+    place = place_ref[0] // 2
+    for offset, ref in enumerate((own_ref, back1_ref, back2_ref, back3_ref)):
+        all_scr[(place + 4 - offset) % 4] = ref[...]
+    changes = [jnp.zeros((DK, DK + DV), f32) for _ in range(HEADS)]
+    for j in range(4):
         for h in range(HEADS):
-            state = states[h]
+            change = changes[h]
 
             @pl.when(place == j)
-            def _(state=state, h=h):
-                prefix_ref[h] = state
-
-            moved, added = compose(state, all_ref[j, h])
-            states[h] = jnp.concatenate([moved[:, :DK], moved[:, DK:] + added], axis=1)
+            def _(change=change, h=h):
+                prefix_ref[h] = change
+
+            changes[h] = then(change, all_scr[j, h])
     for h in range(HEADS):
-        total_ref[h, :, :DK] = (states[h][:, :DK] - eye).astype(bf16)
-        total_ref[h, :, DK:] = states[h][:, DK:].astype(bf16)
-
-
-def run_row(place, gathered):
+        total_ref[h] = changes[h].astype(bf16)
+        before = prefix_ref[h]
+        prefix_ref[h] = jnp.where(odd, then(before, other_ref[h]), before)
+
+
+def run_row(place, own, back1, back2, back3, other):
     return pl.pallas_call(
         row_kernel,
         out_shape=(
-            jax.ShapeDtypeStruct(gathered.shape[1:], f32),
-            jax.ShapeDtypeStruct(gathered.shape[1:], bf16),
+            jax.ShapeDtypeStruct(own.shape, f32),
+            jax.ShapeDtypeStruct(own.shape, bf16),
         ),
-        in_specs=[SMEM, VMEM],
+        in_specs=[SMEM] + [VMEM] * 5,
         out_specs=(VMEM, VMEM),
-        compiler_params=pltpu.CompilerParams(vmem_limit_bytes=GRANT),
+        scratch_shapes=[pltpu.VMEM((4,) + own.shape, bf16)],
+        compiler_params=pltpu.CompilerParams(vmem_limit_bytes=8 * 1024 * 1024),
         name="row",
-    )(place, gathered)
+    )(place, own, back1, back2, back3, other)
 
 
 def finish_kernel(
-    place_ref, rows_ref, start_ref, prefix_ref, summary_ref, reader_ref, local_ref, gate_ref, gain_ref, weight_ref,
-    out_ref, final_ref,
+    place_ref, back1_ref, back2_ref, back3_ref, start_ref, prefix_ref, summary_ref, reader_ref, local_ref, gate_ref,
+    gain_ref, weight_ref, out_ref, final_ref,
 ):
     place = place_ref[0]
-    count = rows_ref.shape[0]
-    eye = (square_iota(DK, 0) == square_iota(DK, 1)).astype(f32)
     entering = []
     for h in range(HEADS):
         state = start_ref[h]
-        for j in range(count - 1):
-            moved, added = compose(state, rows_ref[j, h])
-            state = jnp.where(place > j, moved + added, state)
-        state = state + mm(prefix_ref[h, :, :DK] - eye, state) + prefix_ref[h, :, DK:]
-        final_ref[h] = state + mm(summary_ref[h, :, :DK] - eye, state) + summary_ref[h, :, DK:]
+        for offset, ref in ((3, back3_ref), (2, back2_ref), (1, back1_ref)):
+            state = jnp.where(place >= offset, apply(ref[h], state), state)
+        state = apply(prefix_ref[h], state)
+        final_ref[h] = apply(summary_ref[h], state)
         entering.append(state.astype(bf16))
 
     def tile(i, _):
-        at = pl.ds(pl.multiple_of(i * CHUNK, CHUNK), CHUNK)
+        at = pl.ds(pl.multiple_of(i * TILE, TILE), TILE)
         parts = []
         for h in range(HEADS):
             mixed = mm(reader_ref[h, at, :], entering[h]) + local_ref[h, at, :]
@@ -250,21 +273,21 @@
         out_ref[at, :] = jnp.dot(gated, weight_ref[...], preferred_element_type=f32).astype(bf16)
         return 0
 
-    lax.fori_loop(0, reader_ref.shape[1] // CHUNK, tile, 0)
-
-
-def run_finish(place, rows, start, prefix, summary, reader, local, gate, gain, weight):
+    lax.fori_loop(0, reader_ref.shape[1] // TILE, tile, 0)
+
+
+def run_finish(place, back1, back2, back3, start, prefix, summary, reader, local, gate, gain, weight):
     return pl.pallas_call(
         finish_kernel,
         out_shape=(
             jax.ShapeDtypeStruct((gate.shape[0], weight.shape[1]), bf16),
             jax.ShapeDtypeStruct(start.shape, f32),
         ),
-        in_specs=[SMEM] + [VMEM] * 9,
+        in_specs=[SMEM] + [VMEM] * 11,
         out_specs=(VMEM, VMEM),
         compiler_params=pltpu.CompilerParams(vmem_limit_bytes=GRANT),
         name="finish",
-    )(place, rows, start, prefix, summary, reader, local, gate, gain, weight)
+    )(place, back1, back2, back3, start, prefix, summary, reader, local, gate, gain, weight)
 
 
 def dispatch_kernel(own_ref, mixed_ref, gain_ref, pick_ref, hidden_ref, out_ref):
@@ -296,7 +319,7 @@
     def hidden_of(gate_up):
         return (silu(gate_up[:, :FFE]) * gate_up[:, FFE:]).astype(bf16)
 
-    group = 8
+    group = 32
 
     def step(i, _):
         some = pl.ds(i * group, group)
@@ -353,6 +376,10 @@
         compiler_params=pltpu.CompilerParams(vmem_limit_bytes=GRANT),
         name="combine",
     )(hidden, back, high, low)
+
+
+def turned(size, distance):
+    return [(i, (i + distance) % size) for i in range(size)]
 
 
 def slot_rows(ids, experts):
@@ -411,13 +438,14 @@
         segment, halo, weight, conv_kernel[:, 0], rate_par
     )
     depth = lax.axis_size("z")
-    gathered = lax.all_to_all(
-        jnp.broadcast_to(packed[None], (depth,) + packed.shape), "z", 0, 0, tiled=True
-    )
-    prefix, total = run_row(lax.axis_index("z").reshape(1), gathered)
-    rows = lax.all_gather(total, "x", axis=0)
+    along_z = lax.axis_index("z").reshape(1)
+    other = lax.ppermute(packed, "z", [(i, i ^ 1) for i in range(depth)])
+    both = run_couple(along_z, packed, other)
+    pairs = [lax.ppermute(both, "z", turned(depth, 2 * step)) for step in (1, 2, 3)]
+    prefix, total = run_row(along_z, both, *pairs, other)
+    rows = [lax.ppermute(total, "x", turned(lax.axis_size("x"), step)) for step in (1, 2, 3)]
     partial, final_state = run_finish(
-        lax.axis_index("x").reshape(1), rows, start_state, prefix, summary, reader, local, gate,
+        lax.axis_index("x").reshape(1), *rows, start_state, prefix, summary, reader, local, gate,
         value_gain.reshape(1, -1), output_weight,
     )
     mixed = lax.psum_scatter(partial, CTX, scatter_dimension=0, tiled=True)

time: 344 us -> 313 us (0.910)
  Pallas kernels: 59 us -> 30.2 us
  blocking collectives: 98.8 us -> 83.9 us
  starting transfers between devices: 18.7 us -> 28.8 us
  local copies, waits for them, and re-layouts: 7.57 us -> 15.6 us
  waiting for transfers between devices: 131 us -> 127 us
    all_to_all x1 -> x0, waiting for transfers between devices: 29.1 us -> none  [body(): lax.all_to_all(jnp.broadcast_to(packed[None], (depth,) + packed.shape), '...]
    ppermute x0 -> x7, waiting for transfers between devices: none -> 18.1 us  [the longest x3 8.9 us: body(): lax.ppermute(both, 'z', turned(depth, 2 * step))]
    ppermute x0 -> x7, starting transfers between devices: none -> 17.5 us  [the longest x3 10.2 us: body(): lax.ppermute(both, 'z', turned(depth, 2 * step))]
    all_gather x1 -> x0, blocking collectives: 14.7 us -> none  [body(): rows = lax.all_gather(total, 'x', axis=0)]
    unnamed x12 -> x42, local copies, waits for them, and re-layouts: 4.14 us -> 14.8 us
    pallas_call x1, Pallas kernels: 24.5 us -> 14.1 us  [run_delta(): pl.pallas_call(delta_kernel, out_shape=(jax.ShapeDtypeStruct((rows, HEADS...]
    all_to_all x1 -> x0, starting transfers between devices: 7.25 us -> none  [body(): lax.all_to_all(jnp.broadcast_to(packed[None], (depth,) + packed.shape), '...]
    pallas_call x1, Pallas kernels: 11.5 us -> 5.24 us  [run_expert(): pl.pallas_call(expert_kernel, out_shape=jax.ShapeDtypeStruct(rows.shape,...]
  transfers between devices with their start and end apart: 5 -> 11, of which waited for: 4 -> 8; matrix products, arithmetic and copies ran while one was open for 4% -> 3% of each run, Pallas kernels for 0% -> 0%
where the time goes in v2:
time: 313 us; the launch traced here: 312 us
  waiting for transfers between devices  127 us (41%)
  blocking collectives  83.9 us (27%)
  Pallas kernels  30.2 us (10%)
  starting transfers between devices  28.8 us (9%)
  local copies, waits for them, and re-layouts  15.6 us (5%)
  between operations  14.3 us (5%)
  other arithmetic  11.8 us (4%)
    all_to_all x1, blocking collectives, body(): lax.all_to_all(outgoing.reshape(experts, 40, half), EXP, 0, 0, tiled=True)  70.8 us
    all_to_all x1, waiting for transfers between devices, body(): back = lax.all_to_all(made, EXP, 0, 0, tiled=True)  62 us
    reduce_scatter x1, waiting for transfers between devices, body(): mixed = lax.psum_scatter(partial, CTX, scatter_dimension=0, tiled=True)  34.9 us
    unnamed x42, local copies, waits for them, and re-layouts  14.8 us
    pallas_call x1, Pallas kernels, run_delta(): pl.pallas_call(delta_kernel, out_shape=(jax.ShapeDtypeStruct((rows, HEADS...  14.1 us
    all_gather x1, blocking collectives, body(): halo = lax.all_gather(last_rows, CTX, axis=0)[-1]  13.2 us
    all_gather x1, waiting for transfers between devices, body(): segment = lax.all_gather(normed, CTX, axis=0, tiled=True)  12 us
    ppermute x3, starting transfers between devices, body(): lax.ppermute(both, 'z', turned(depth, 2 * step))  10.2 us
  transfers between devices with their start and end apart: 11, of which 8 were waited for; matrix products, arithmetic and copies ran while one was open for 3% of the time, Pallas kernels for 0%

profile of v2, /device:TPU:24, one launch (start us, length us, event | category | flops | bytes accessed | tf_op | source)
XLA Modules:
  0.0 311.9 jit_solution(1562530196909787173)
XLA Ops:
  7.2 1.2 fusion.1
  8.4 2.0 fusion.3
  10.6 0.8 slice.9
  11.3 3.8 %collective-permute-start = (bf16[8,2048]{1,0:T(8,128)(2,1)S(1)}, bf16[8,2048]{1,0:T(8,128)(2,1)S(1)}, u32[]{:S(2)}, u32[]{:S(2)}) collective-permute-start(bf16[8,2048]{1,0:T(8,128)(2,1)S(1)} %slice.9), channel_id=1, source_target_pairs={{0,1},{1,2},{2,3},{3,4},{4,5},{5,6},{6,7},{7,8},{8,9},{9,10},{10,1... | collective-permute-start | bytes 98312 | tf_op jit(solution)/shard_map/ppermute | solution.py:420
  15.1 1.0 copy.22
  16.2 0.1 pad.14.clone
  16.3 0.7 fusion.13
  17.0 4.4 %maximum_maximum_fusion.weight_ref = bf16[2048,896]{1,0:T(8,128)(2,1)} fusion(bf16[2048,4]{1,0:T(8,128)(2,1)S(1)} %bitcast.36, bf16[2048,768]{1,0:T(8,128)(2,1)} %param.17, bf16[896]{0:T(1024)(128)(2,1)S(1)} %pad.14.clone), kind=kLoop, calls=%fused_computation.4 | loop fusion | flops 11010048 | bytes 6833920 | tf_op jit(solution)/shard_map/concatenate | solution.py:422
  21.5 13.2 %all-gather = bf16[64,2048]{1,0:T(8,128)(2,1)S(1)} all-gather(bf16[8,2048]{1,0:T(8,128)(2,1)S(1)} %collective-permute-done), channel_id=2, replica_groups=mesh['y'=4,'core'=2,'x'=4,'z'=8] {'y','core'}, dimensions={0}, use_global_device_ids=true | all-gather | bytes 294912 | tf_op jit(solution)/shard_map/all_gather | solution.py:421
  34.7 12.0 %all-gather.3.cloned.1.call-done.seg_ref = bf16[1024,2048]{1,0:T(8,128)(2,1)} async-done(((bf16[128,2048]{1,0:T(8,128)(2,1)}), bf16[1024,2048]{1,0:T(8,128)(2,1)}) %all-gather.3.cloned.1.call-update) | async-done | bytes 4194320 | tf_op jit(solution)/shard_map/all_gather | solution.py:419
  46.7 2.0 copy-done.4
  48.7 2.2 copy-done.16
  50.9 14.1 %delta.1 = (bf16[1024,256]{1,0:T(8,128)(2,1)S(1)}, bf16[2,1024,128]{2,1,0:T(8,128)(2,1)S(1)}, f32[2,1024,128]{2,1,0:T(8,128)S(1)}, f32[2,128,256]{2,1,0:T(8,128)S(1)}, bf16[2,128,256]{2,1,0:T(8,128)(2,1)}) custom-call(bf16[1024,2048]{1,0:T(8,128)(2,1)S(1)} %copy-done.16, bf16[8,2048]{1,0:T(8,128)(2,1)S(1)} %slice.10.halo_ref, ...), custom_call_target="tpu_custom_call" | custom-call | flops 12000000000 | bytes 12000000 | tf_op jit(solution)/shard_map/delta/pallas_call | solution.py:167
  65.0 1.6 collective-permute-start.1
  66.6 4.2 %collective-permute-done.1.other_ref = bf16[2,128,256]{2,1,0:T(8,128)(2,1)S(1)} collective-permute-done((bf16[2,128,256]{2,1,0:T(8,128)(2,1)}, bf16[2,128,256]{2,1,0:T(8,128)(2,1)S(1)}, u32[]{:S(2)}, u32[]{:S(2)}) %collective-permute-start.1) | collective-permute-done | bytes 131104 | tf_op jit(solution)/shard_map/ppermute | solution.py:442
  70.8 1.1 couple.1.own_ref
  71.9 3.0 collective-permute-start.2
  75.0 3.9 %collective-permute-start.3 = (bf16[2,128,256]{2,1,0:T(8,128)(2,1)S(1)}, bf16[2,128,256]{2,1,0:T(8,128)(2,1)S(1)}, u32[]{:S(2)}, u32[]{:S(2)}) collective-permute-start(bf16[2,128,256]{2,1,0:T(8,128)(2,1)S(1)} %couple.1.own_ref), channel_id=1, source_target_pairs={{0,4},{1,5},{2,6},{3,7},{4,0},{5,1},{6,2},{7,3},{8,12},{9,13},{10,... | collective-permute-start | bytes 393224 | tf_op jit(solution)/shard_map/ppermute | solution.py:444
  78.9 3.3 %collective-permute-start.4 = (bf16[2,128,256]{2,1,0:T(8,128)(2,1)S(1)}, bf16[2,128,256]{2,1,0:T(8,128)(2,1)S(1)}, u32[]{:S(2)}, u32[]{:S(2)}) collective-permute-start(bf16[2,128,256]{2,1,0:T(8,128)(2,1)S(1)} %couple.1.own_ref), channel_id=1, source_target_pairs={{0,6},{1,7},{2,0},{3,1},{4,2},{5,3},{6,4},{7,5},{8,14},{9,15},{10,... | collective-permute-start | bytes 393224 | tf_op jit(solution)/shard_map/ppermute | solution.py:444
  82.2 5.6 %collective-permute-done.3.back2_ref = bf16[2,128,256]{2,1,0:T(8,128)(2,1)S(1)} collective-permute-done((bf16[2,128,256]{2,1,0:T(8,128)(2,1)S(1)}, bf16[2,128,256]{2,1,0:T(8,128)(2,1)S(1)}, u32[]{:S(2)}, u32[]{:S(2)}) %collective-permute-start.3) | collective-permute-done | bytes 131104 | tf_op jit(solution)/shard_map/ppermute | solution.py:444
  87.8 3.3 %collective-permute-done.4.back3_ref = bf16[2,128,256]{2,1,0:T(8,128)(2,1)S(1)} collective-permute-done((bf16[2,128,256]{2,1,0:T(8,128)(2,1)S(1)}, bf16[2,128,256]{2,1,0:T(8,128)(2,1)S(1)}, u32[]{:S(2)}, u32[]{:S(2)}) %collective-permute-start.4) | collective-permute-done | bytes 131104 | tf_op jit(solution)/shard_map/ppermute | solution.py:444
  91.1 2.0 row.1
  93.1 0.7 copy-done.11
  93.8 1.5 collective-permute-start.5
  95.2 2.6 collective-permute-start.6
  97.8 1.6 collective-permute-start.7
  99.4 1.3 collective-permute-done.5.back1_ref
  100.7 3.6 %collective-permute-done.6.back2_ref = bf16[2,128,256]{2,1,0:T(8,128)(2,1)} collective-permute-done((bf16[2,128,256]{2,1,0:T(8,128)(2,1)}, bf16[2,128,256]{2,1,0:T(8,128)(2,1)}, u32[]{:S(2)}, u32[]{:S(2)}) %collective-permute-start.6) | collective-permute-done | bytes 131104 | tf_op jit(solution)/shard_map/ppermute | solution.py:446
  104.4 0.9 copy-done.12
  105.3 0.9 copy-done.13
  106.2 4.1 %finish.1 = (bf16[1024,2048]{1,0:T(8,128)(2,1)S(1)}, f32[2,128,128]{2,1,0:T(8,128)}) custom-call(s32[1]{0:T(128)} %bitcast.1.place_ref, bf16[2,128,256]{2,1,0:T(8,128)(2,1)S(1)} %collective-permute-done.5.back1_ref, bf16[2,128,256]{2,1,0:T(8,128)(2,1)} %collective-permute-done.6.back2_ref, bf16[2,128,256]{2,1,0:T(8,128)(2,1)} %collective-permute-done.7.back3_ref, ...), custom_call_target="tpu_custom_call" | custom-call | tf_op jit(solution)/shard_map/finish/pallas_call | solution.py:280
  110.4 1.9 copy-done.2
  112.4 0.2 fusion.6
  112.6 1.5 fusion
  114.1 0.1 convert_element_type.25.pick_ref
  114.3 34.9 %reduce-scatter.2.cloned.1.call-done.mixed_ref = bf16[128,2048]{1,0:T(8,128)(2,1)} async-done(((bf16[1024,2048]{1,0:T(8,128)(2,1)}), bf16[128,2048]{1,0:T(8,128)(2,1)}) %reduce-scatter.2.cloned.1.call-update) | async-done | bytes 524304 | tf_op jit(solution)/shard_map/reduce_scatter | solution.py:451
  149.2 1.2 copy-done.10
  150.4 1.1 dispatch.1
  151.6 70.8 %all_to_all.10.rows_ref = bf16[32,40,1024]{2,1,0:T(8,128)(2,1)S(1)} all-to-all(bf16[32,40,1024]{2,1,0:T(8,128)(2,1)S(1)} %bitcast.31), channel_id=1, replica_groups=mesh['y'=4,'core'=2,'x'=4,'z'=8] {'x','z'}, dimensions={0} | all-to-all | bytes 5242880 | tf_op jit(solution)/shard_map/all_to_all | solution.py:466
  222.3 5.2 %expert.1 = bf16[32,40,1024]{2,1,0:T(8,128)(2,1)S(1)} custom-call(bf16[32,40,1024]{2,1,0:T(8,128)(2,1)S(1)} %all_to_all.10.rows_ref, bf16[2048,1024]{1,0:T(8,128)(2,1)S(1)} %bitcast.30, bf16[512,2048]{1,0:T(8,128)(2,1)S(1)} %bitcast.32), custom_call_target="tpu_custom_call" | custom-call | tf_op jit(solution)/shard_map/expert/pallas_call | solution.py:349
  227.6 1.5 copy-done
  229.1 7.5 %all-to-all-start.1 = ((bf16[32,40,1024]{2,1,0:T(8,128)(2,1)}), bf16[32,40,1024]{2,1,0:T(8,128)(2,1)S(1)}, u32[]{:S(2)}, u32[]{:S(2)}) async-start(bf16[32,40,1024]{2,1,0:T(8,128)(2,1)} %copy-done), calls=%async_computation.2 | async-start | bytes 5242880 | tf_op jit(solution)/shard_map/all_to_all | solution.py:468
  236.6 0.7 select_reduce_fusion
  237.3 0.9 subtract_convert_fusion
  238.2 62.0 %all-to-all-done.1 = bf16[32,40,1024]{2,1,0:T(8,128)(2,1)S(1)} async-done(((bf16[32,40,1024]{2,1,0:T(8,128)(2,1)}), bf16[32,40,1024]{2,1,0:T(8,128)(2,1)S(1)}, u32[]{:S(2)}, u32[]{:S(2)}) %all-to-all-start.1) | async-done | bytes 2621472 | tf_op jit(solution)/shard_map/all_to_all | solution.py:468
  300.3 1.1 copy-done.5
  301.4 1.2 copy-done.9
  302.6 2.5 combine.1
  (50 shorter events, 0.3 us)
Async XLA Ops:
  7.2 39.5 %all-gather.3.cloned.1.call-start = ((), (), s32[]{:S(2)}) async-start(), calls=%async_computation.3 | async-start | bytes 4718592 | tf_op jit(solution)/shard_map/all_gather | solution.py:419
  10.5 138.7 %reduce-scatter.2.cloned.1.call-start = ((), (), s32[]{:S(2)}) async-start(), calls=%async_computation.4 | async-start | bytes 4718592 | tf_op jit(solution)/shard_map/reduce_scatter | solution.py:451
  11.3 10.2 %collective-permute-start = (bf16[8,2048]{1,0:T(8,128)(2,1)S(1)}, bf16[8,2048]{1,0:T(8,128)(2,1)S(1)}, u32[]{:S(2)}, u32[]{:S(2)}) collective-permute-start(bf16[8,2048]{1,0:T(8,128)(2,1)S(1)} %slice.9), channel_id=1, source_target_pairs={{0,1},{1,2},{2,3},{3,4},{4,5},{5,6},{6,7},{7,8},{8,9},{9,10},{10,1... | collective-permute-start | bytes 98312 | tf_op jit(solution)/shard_map/ppermute | solution.py:420
  17.0 4.5 %copy-start.18 = (f32[4,1,512]{2,1,0:T(1,128)S(1)}, f32[4,1,512]{2,1,0:T(1,128)}, u32[]{:S(2)}) copy-start(f32[4,1,512]{2,1,0:T(1,128)} %param.19) | copy-start | bytes 24580
  46.7 2.0 copy-start.4
  48.7 2.2 copy-start.16
  50.9 53.4 %copy-start.7 = (bf16[256,2048]{1,0:T(8,128)(2,1)S(1)}, bf16[256,2048]{1,0:T(8,128)(2,1)}, u32[]{:S(2)}) copy-start(bf16[256,2048]{1,0:T(8,128)(2,1)} %weight_ref.1) | copy-start | bytes 3145732
  50.9 53.4 %copy-start.15 = (f32[128]{0:T(128)S(1)}, f32[128]{0:T(128)}, u32[]{:S(2)}) copy-start(f32[128]{0:T(128)} %param.22) | copy-start | bytes 1540
  65.0 5.9 %collective-permute-start.1 = (bf16[2,128,256]{2,1,0:T(8,128)(2,1)}, bf16[2,128,256]{2,1,0:T(8,128)(2,1)S(1)}, u32[]{:S(2)}, u32[]{:S(2)}) collective-permute-start(bf16[2,128,256]{2,1,0:T(8,128)(2,1)} %get-tuple-element.13.own_ref), channel_id=1, source_target_pairs={{0,1},{1,0},{2,3},{3,2},{4,5},{5,4},{6,7},{7,6},{8,9},{9,8},{10,11... | collective-permute-start | bytes 393224 | tf_op jit(solution)/shard_map/ppermute | solution.py:442
  71.9 10.2 %collective-permute-start.2 = (bf16[2,128,256]{2,1,0:T(8,128)(2,1)S(1)}, bf16[2,128,256]{2,1,0:T(8,128)(2,1)S(1)}, u32[]{:S(2)}, u32[]{:S(2)}) collective-permute-start(bf16[2,128,256]{2,1,0:T(8,128)(2,1)S(1)} %couple.1.own_ref), channel_id=1, source_target_pairs={{0,2},{1,3},{2,4},{3,5},{4,6},{5,7},{6,0},{7,1},{8,10},{9,11},{10,... | collective-permute-start | bytes 393224 | tf_op jit(solution)/shard_map/ppermute | solution.py:444
  75.0 12.9 %collective-permute-start.3 = (bf16[2,128,256]{2,1,0:T(8,128)(2,1)S(1)}, bf16[2,128,256]{2,1,0:T(8,128)(2,1)S(1)}, u32[]{:S(2)}, u32[]{:S(2)}) collective-permute-start(bf16[2,128,256]{2,1,0:T(8,128)(2,1)S(1)} %couple.1.own_ref), channel_id=1, source_target_pairs={{0,4},{1,5},{2,6},{3,7},{4,0},{5,1},{6,2},{7,3},{8,12},{9,13},{10,... | collective-permute-start | bytes 393224 | tf_op jit(solution)/shard_map/ppermute | solution.py:444
  78.9 12.2 %collective-permute-start.4 = (bf16[2,128,256]{2,1,0:T(8,128)(2,1)S(1)}, bf16[2,128,256]{2,1,0:T(8,128)(2,1)S(1)}, u32[]{:S(2)}, u32[]{:S(2)}) collective-permute-start(bf16[2,128,256]{2,1,0:T(8,128)(2,1)S(1)} %couple.1.own_ref), channel_id=1, source_target_pairs={{0,6},{1,7},{2,0},{3,1},{4,2},{5,3},{6,4},{7,5},{8,14},{9,15},{10,... | collective-permute-start | bytes 393224 | tf_op jit(solution)/shard_map/ppermute | solution.py:444
  93.1 0.7 copy-start.11
  93.8 6.9 %collective-permute-start.5 = (bf16[2,128,256]{2,1,0:T(8,128)(2,1)}, bf16[2,128,256]{2,1,0:T(8,128)(2,1)S(1)}, u32[]{:S(2)}, u32[]{:S(2)}) collective-permute-start(bf16[2,128,256]{2,1,0:T(8,128)(2,1)} %get-tuple-element.14), channel_id=1, source_target_pairs={{0,8},{8,16},{16,24},{24,0},{1,9},{9,17},{17,25},{25,1},{2,10},{10... | collective-permute-start | bytes 393224 | tf_op jit(solution)/shard_map/ppermute | solution.py:446
  95.2 9.1 %collective-permute-start.6 = (bf16[2,128,256]{2,1,0:T(8,128)(2,1)}, bf16[2,128,256]{2,1,0:T(8,128)(2,1)}, u32[]{:S(2)}, u32[]{:S(2)}) collective-permute-start(bf16[2,128,256]{2,1,0:T(8,128)(2,1)} %get-tuple-element.14), channel_id=1, source_target_pairs={{0,16},{8,24},{16,0},{24,8},{1,17},{9,25},{17,1},{25,9},{2,18},{10... | collective-permute-start | bytes 393224 | tf_op jit(solution)/shard_map/ppermute | solution.py:446
  97.8 6.5 %collective-permute-start.7 = (bf16[2,128,256]{2,1,0:T(8,128)(2,1)}, bf16[2,128,256]{2,1,0:T(8,128)(2,1)}, u32[]{:S(2)}, u32[]{:S(2)}) collective-permute-start(bf16[2,128,256]{2,1,0:T(8,128)(2,1)} %get-tuple-element.14), channel_id=1, source_target_pairs={{0,24},{8,0},{16,8},{24,16},{1,25},{9,1},{17,9},{25,17},{2,26},{10... | collective-permute-start | bytes 393224 | tf_op jit(solution)/shard_map/ppermute | solution.py:446
  104.3 1.0 copy-start.12
  105.3 0.9 copy-start.13
  106.2 6.1 %copy-start.17 = (s32[1,128,4]{1,2,0:T(4,128)S(1)}, s32[1,128,4]{1,2,0:T(4,128)}, u32[]{:S(2)}) copy-start(s32[1,128,4]{1,2,0:T(4,128)} %param.28) | copy-start | bytes 6148
  110.4 1.9 copy-start.2
  112.3 36.9 %copy-start.1 = (bf16[1,128,2048]{2,1,0:T(8,128)(2,1)S(1)}, bf16[1,128,2048]{2,1,0:T(8,128)(2,1)}, u32[]{:S(2)}) copy-start(bf16[1,128,2048]{2,1,0:T(8,128)(2,1)} %param.15) | copy-start | bytes 1572868
  112.3 36.9 %copy-start.14 = (f32[2048]{0:T(1024)S(1)}, f32[2048]{0:T(1024)}, u32[]{:S(2)}) copy-start(f32[2048]{0:T(1024)} %param.25) | copy-start | bytes 24580
  114.3 108.1 %copy-start.6 = (bf16[1,512,2048]{2,1,0:T(8,128)(2,1)S(1)}, bf16[1,512,2048]{2,1,0:T(8,128)(2,1)}, u32[]{:S(2)}) copy-start(bf16[1,512,2048]{2,1,0:T(8,128)(2,1)} %param.27) | copy-start | bytes 6291460
  149.2 73.1 %copy-start.3 = (bf16[1,2048,1024]{2,1,0:T(8,128)(2,1)S(1)}, bf16[1,2048,1024]{2,1,0:T(8,128)(2,1)}, u32[]{:S(2)}) copy-start(bf16[1,2048,1024]{2,1,0:T(8,128)(2,1)} %param.26) | copy-start | bytes 12582916
  149.2 1.2 copy-start.10
  151.6 70.8 %copy-start.8 = (f32[128,2048]{1,0:T(8,128)}, f32[128,2048]{1,0:T(8,128)S(1)}, u32[]{:S(2)}) copy-start(f32[128,2048]{1,0:T(8,128)S(1)} %get-tuple-element.21.hidden_ref) | copy-start | bytes 3145732
  227.6 1.5 copy-start
  229.1 7.5 %copy-start.19 = (f32[1,128,4]{1,2,0:T(4,128)S(1)}, f32[1,128,4]{1,2,0:T(4,128)}, u32[]{:S(2)}) copy-start(f32[1,128,4]{1,2,0:T(4,128)} %param.29) | copy-start | bytes 6148
  229.1 71.2 %all-to-all-start.1 = ((bf16[32,40,1024]{2,1,0:T(8,128)(2,1)}), bf16[32,40,1024]{2,1,0:T(8,128)(2,1)S(1)}, u32[]{:S(2)}, u32[]{:S(2)}) async-start(bf16[32,40,1024]{2,1,0:T(8,128)(2,1)} %copy-done), calls=%async_computation.2 | async-start | bytes 5242880 | tf_op jit(solution)/shard_map/all_to_all | solution.py:468
  300.3 1.1 copy-start.5
  301.4 1.2 copy-start.9
Sparse Core Ops, SparseCore 0:
  10.6 35.9 all-gather.2
  112.4 36.7 reduce-scatter.1
